TPU v7x, 256 devices: a whole 4x4x8 slice. The times are simulated.
256 devices in a mesh: dp: 16 (over x, y_hi, core), space: 16 (over z, y_lo).
Axes of the slice: x: 4, y: 4 (y_hi: 2, y_lo: 2; y = y_hi * 2 + y_lo), z: 8, core: 2. Of those that a mesh axis runs over, the one named last changes fastest.
Arguments:
- fine_map: bfloat16 [256, 80, 32, 128], P('dp', None, 'space'), may hold values from -6 to 6
- coarse_map: bfloat16 [256, 224, 16, 64], P('dp', None, 'space'), may hold values from -6 to 6
- fine_cotan: bfloat16 [256, 384, 32, 128], P('dp', None, 'space'), may hold values from -0.005859375 to 0.005859375
- coarse_cotan: bfloat16 [256, 384, 16, 64], P(('dp', 'space')), may hold values from -0.01171875 to 0.01171875
- lateral_fine: bfloat16 [80, 384], replicated, may hold values from -0.625 to 0.625
- lateral_coarse: bfloat16 [224, 384], replicated, may hold values from -0.375 to 0.375
- point_fine: bfloat16 [384, 384], replicated, may hold values from -0.3125 to 0.3125
- point_coarse: bfloat16 [384, 384], replicated, may hold values from -0.3125 to 0.3125
- kernel_fine: float32 [3, 3, 384], replicated, may hold values from -2 to 2
- kernel_coarse: float32 [3, 3, 384], replicated, may hold values from -2 to 2
- joining: float32 [4], replicated, may hold values from 0.5 to 2
Outputs:
- grad_lateral_fine: float32 [80, 384], replicated
- grad_lateral_coarse: float32 [224, 384], replicated
- grad_point_fine: float32 [384, 384], replicated
- grad_point_coarse: float32 [384, 384], replicated
- grad_kernel_fine: float32 [3, 3, 384], replicated
- grad_kernel_coarse: float32 [3, 3, 384], replicated
- grad_joining: float32 [4], replicated
All inputs are finite; a program needn't handle non-finite values.
Results may differ from a plain program's by a relative error of at most 0.025.
Values may be sent and summed in bfloat16 or wider, within the bound.
No kernel may reach another device: no remote copies, remote signals or barrier semaphores. Data moves between devices by JAX's collectives and lax.ppermute only.
A program may use at most 128 MiB of HBM per device.

v0:
```python
import jax
import jax.numpy as jnp
from jax import lax
from jax.sharding import PartitionSpec as P

EPSILON = 0.0001


def extended(cells, sides, width):
    for axis, dim in sides:
        count = lax.axis_size(axis)
        ends = count - 1
        head = lax.slice_in_dim(cells, 0, width, axis=dim)
        tail = lax.slice_in_dim(cells, cells.shape[dim] - width, cells.shape[dim], axis=dim)
        cells = jnp.concatenate(
            [
                lax.ppermute(tail, axis, [(i, (i + 1) % count) for i in range(ends)]),
                cells,
                lax.ppermute(head, axis, [((i + 1) % count, i) for i in range(ends)]),
            ],
            axis=dim,
        )
    return cells


def swish(values):
    return values * jax.nn.sigmoid(values)


def swish_slope(values):
    logistic = jax.nn.sigmoid(values)
    return logistic * (1.0 + values * (1.0 - logistic))


def project(weight, values):
    return jnp.einsum("cf,bcrw->bfrw", weight, values, preferred_element_type=jnp.float32)


def project_back(weight, cotangent):
    return jnp.einsum("cf,bfrw->bcrw", weight, cotangent, preferred_element_type=jnp.float32)


def weight_grad(values, cotangent):
    return jnp.einsum("bcrw,bfrw->cf", values, cotangent, preferred_element_type=jnp.float32)


def upsample(values):
    return jnp.repeat(jnp.repeat(values, 2, axis=2), 2, axis=3)


def pool_sum(values):
    shaped = values.reshape(
        values.shape[0], values.shape[1], values.shape[2] // 2, 2, values.shape[3] // 2, 2
    )
    return shaped.sum(axis=(3, 5))


def zero_rows(values):
    return jnp.pad(values, ((0, 0), (0, 0), (1, 1), (0, 0)))


def add_rim(values):
    return extended(values, (("space", 2),), 1)


def to_batch(values):
    return lax.all_to_all(values, "space", split_axis=0, concat_axis=2, tiled=True)


def to_rows(values):
    return lax.all_to_all(values, "space", split_axis=2, concat_axis=0, tiled=True)


def widen(padded):
    return jnp.pad(padded, ((0, 0), (0, 0), (0, 0), (1, 1)))


def spread(padded, kernel, reverse):
    row_count = padded.shape[2] - 2
    col_count = padded.shape[3]
    widened = widen(padded)
    running = None
    for row_off in range(3):
        for col_off in range(3):
            row_start = 2 - row_off if reverse else row_off
            col_start = 2 - col_off if reverse else col_off
            term = kernel[row_off, col_off][None, :, None, None] * widened[
                :, :, row_start : row_start + row_count, col_start : col_start + col_count
            ].astype(jnp.float32)
            running = term if running is None else running + term
    return running


def kernel_grad(cotangent, padded):
    row_count = padded.shape[2] - 2
    col_count = padded.shape[3]
    widened = widen(padded)
    stacked = []
    for row_off in range(3):
        row_list = []
        for col_off in range(3):
            window = widened[:, :, row_off : row_off + row_count, col_off : col_off + col_count]
            row_list.append(
                jnp.sum(cotangent.astype(jnp.float32) * window.astype(jnp.float32), axis=(0, 2, 3))
            )
        stacked.append(jnp.stack(row_list))
    return jnp.stack(stacked)


def body(
    fine_map,
    coarse_map,
    fine_cotan,
    coarse_cotan,
    lateral_fine,
    lateral_coarse,
    point_fine,
    point_coarse,
    kernel_fine,
    kernel_coarse,
    joining,
):
    halves = jnp.bfloat16
    floats = jnp.float32
    fine_own, fine_up, coarse_own, coarse_down = (joining[0], joining[1], joining[2], joining[3])
    fine_total = fine_own + fine_up + EPSILON
    coarse_total = coarse_own + coarse_down + EPSILON
    coarse_input = to_batch(coarse_map)
    proj_coarse = project(lateral_coarse, coarse_input).astype(halves)
    proj_lifted = to_rows(proj_coarse)
    proj_fine = project(lateral_fine, fine_map).astype(halves)
    upsampled = upsample(proj_lifted)
    joined_fine = (
        fine_own * proj_fine.astype(floats) + fine_up * upsampled.astype(floats)
    ) / fine_total
    active_fine = swish(joined_fine).astype(halves)
    padded_fine = add_rim(active_fine)
    depth_fine = spread(padded_fine, kernel_fine, False).astype(halves)
    output_fine = project(point_fine, depth_fine).astype(halves)
    pooled_fine = (0.25 * pool_sum(output_fine.astype(floats))).astype(halves)
    pooled_batch = to_batch(pooled_fine)
    joined_coarse = (
        coarse_own * proj_coarse.astype(floats) + coarse_down * pooled_batch.astype(floats)
    ) / coarse_total
    active_coarse = swish(joined_coarse).astype(halves)
    padded_coarse = zero_rows(active_coarse)
    depth_coarse = spread(padded_coarse, kernel_coarse, False).astype(halves)
    point_coarse_grad = weight_grad(depth_coarse, coarse_cotan)
    back_coarse = project_back(point_coarse, coarse_cotan).astype(halves)
    kernel_coarse_grad = kernel_grad(back_coarse, padded_coarse)
    slope_coarse = spread(zero_rows(back_coarse), kernel_coarse, True) * swish_slope(joined_coarse)
    own_coarse_grad = (
        jnp.sum(slope_coarse * (proj_coarse.astype(floats) - joined_coarse)) / coarse_total
    )
    down_coarse_grad = (
        jnp.sum(slope_coarse * (pooled_batch.astype(floats) - joined_coarse)) / coarse_total
    )
    pooled_back = (coarse_down / coarse_total * slope_coarse).astype(halves)
    own_back = (coarse_own / coarse_total * slope_coarse).astype(halves)
    mixed_cotan = (
        fine_cotan.astype(floats) + 0.25 * upsample(to_rows(pooled_back)).astype(floats)
    ).astype(halves)
    point_fine_grad = weight_grad(depth_fine, mixed_cotan)
    back_fine = project_back(point_fine, mixed_cotan).astype(halves)
    kernel_fine_grad = kernel_grad(back_fine, padded_fine)
    slope_fine = spread(add_rim(back_fine), kernel_fine, True) * swish_slope(joined_fine)
    own_fine_grad = jnp.sum(slope_fine * (proj_fine.astype(floats) - joined_fine)) / fine_total
    up_fine_grad = jnp.sum(slope_fine * (upsampled.astype(floats) - joined_fine)) / fine_total
    lateral_back = (fine_own / fine_total * slope_fine).astype(halves)
    lateral_fine_grad = weight_grad(fine_map, lateral_back)
    up_back = (fine_up / fine_total * pool_sum(slope_fine)).astype(halves)
    lateral_coarse_grad = weight_grad(coarse_input, own_back)
    lateral_coarse_grad = lateral_coarse_grad + weight_grad(coarse_input, to_batch(up_back))
    joining_grad = jnp.stack([own_fine_grad, up_fine_grad, own_coarse_grad, down_coarse_grad])
    return lax.psum(
        (
            lateral_fine_grad,
            lateral_coarse_grad,
            point_fine_grad,
            point_coarse_grad,
            kernel_fine_grad,
            kernel_coarse_grad,
            joining_grad,
        ),
        ("dp", "space"),
    )


def solution(mesh):
    return jax.shard_map(
        body,
        mesh=mesh,
        in_specs=(
            P("dp", None, "space", None),
            P("dp", None, "space", None),
            P("dp", None, "space", None),
            P(("dp", "space"), None, None, None),
            P(),
            P(),
            P(),
            P(),
            P(),
            P(),
            P(),
        ),
        out_specs=(P(), P(), P(), P(), P(), P(), P()),
        check_vma=False,
    )
```

profile of v0, /device:TPU:1, one launch (start us, length us, event | category | flops | bytes accessed | tf_op | source)
XLA Modules:
  0.0 660.0 jit_solution(14477227337791057524)
XLA Ops:
  7.2 25.9 %all_to_all.57 = bf16[16,224,1,64]{1,3,2,0:T(8,128)(2,1)S(1)} all-to-all(bf16[16,224,1,64]{1,3,2,0:T(8,128)(2,1)} %param.12), channel_id=1, replica_groups=mesh['dp'=16,'space'=16] {'space'}, dimensions={0} | all-to-all | bytes 917504 | tf_op jit(solution)/shard_map/all_to_all | solution.py:67
  33.9 2.2 convolution_convert_fusion.1
  36.2 4.8 all-to-all-start.1
  42.9 18.5 %all-to-all-done.1 = bf16[1,384,16,64]{1,3,0,2:T(8,128)(2,1)S(1)} async-done(((bf16[1,384,16,64]{1,3,0,2:T(8,128)(2,1)}), bf16[1,384,16,64]{1,3,0,2:T(8,128)(2,1)S(1)}, u32[]{:S(2)}, u32[]{:S(2)}) %all-to-all-start.1) | async-done | bytes 786464 | tf_op jit(solution)/shard_map/all_to_all | solution.py:71
  61.6 2.8 broadcast_in_dim.14
  64.3 5.3 convert_element_type.335
  69.6 2.9 broadcast_multiply_fusion
  72.6 4.3 multiply_convert_fusion.1
  77.4 1.3 collective-permute-start.1
  78.7 4.6 collective-permute-start
  83.3 28.5 %collective-permute-done.1 = bf16[16,384,1,128]{1,3,2,0:T(8,128)(2,1)S(1)} collective-permute-done((bf16[16,384,1,128]{1,3,2,0:T(8,128)(2,1)S(1)}, bf16[16,384,1,128]{1,3,2,0:T(8,128)(2,1)S(1)}, u32[]{:S(2)}, u32[]{:S(2)}) %collective-permute-start.1) | collective-permute-done | bytes 1572896 | tf_op jit(solution)/shard_map/ppermute | solution.py:19
  111.8 36.2 %collective-permute-done = bf16[16,384,1,128]{1,3,2,0:T(8,128)(2,1)S(1)} collective-permute-done((bf16[16,384,1,128]{1,3,2,0:T(8,128)(2,1)S(1)}, bf16[16,384,1,128]{1,3,2,0:T(8,128)(2,1)S(1)}, u32[]{:S(2)}, u32[]{:S(2)}) %collective-permute-start) | collective-permute-done | bytes 1572896 | tf_op jit(solution)/shard_map/ppermute | solution.py:17
  148.0 3.5 fusion.5
  151.6 7.7 %fusion.14 = bf16[16,384,2,128]{1,3,2,0:T(8,128)(2,1)S(1)} fusion(bf16[16,384,2,128]{1,3,2,0:T(8,128)(2,1)S(1)} %get-tuple-element.72, f32[384]{0:T(512)S(1)} %get-tuple-element.43, f32[384]{0:T(512)S(1)} %get-tuple-element.44, f32[384]{0:T(512)S(1)} %get-tuple-element.37, f32[384]{0:T(512)S(1)} %get-tuple-element.38, f32[384]{0:T(512)S(1)} %get-tuple-element.39, ...), kind=kLoop, calls=%fused_computation.37 | loop fusion | flops 45613056 | bytes 28325376 | tf_op jit(solution)/shard_map/convert_element_type | solution.py:138
  159.4 2.1 convert_reduce_fusion
  161.5 2.0 bitcast_reduce_fusion.1
  163.5 1.4 fusion.84
  164.9 9.1 %all-to-all-start.2 = ((bf16[16,384,1,64]{1,3,2,0:T(8,128)(2,1)}), bf16[16,384,1,64]{1,3,2,0:T(8,128)(2,1)S(1)}, u32[]{:S(2)}, u32[]{:S(2)}) async-start(bf16[16,384,1,64]{1,3,2,0:T(8,128)(2,1)} %fusion.84), calls=%async_computation.2 | async-start | bytes 1572864 | tf_op jit(solution)/shard_map/all_to_all | solution.py:67
  177.8 17.1 %all-to-all-done.2 = bf16[16,384,1,64]{1,3,2,0:T(8,128)(2,1)S(1)} async-done(((bf16[16,384,1,64]{1,3,2,0:T(8,128)(2,1)}), bf16[16,384,1,64]{1,3,2,0:T(8,128)(2,1)S(1)}, u32[]{:S(2)}, u32[]{:S(2)}) %all-to-all-start.2) | async-done | bytes 786464 | tf_op jit(solution)/shard_map/all_to_all | solution.py:67
  195.7 7.4 %fusion.45 = (f32[]{:T(128)}, f32[]{:T(128)}, f32[1,384,16,64]{1,3,2,0:T(8,128)S(1)}, bf16[1,384,16,64]{1,3,2,0:T(8,128)(2,1)}) fusion(bf16[16,64,384]{2,1,0:T(8,128)(2,1)} %convolution_convert_fusion.1, f32[]{:T(128)S(6)} %add.166, bf16[16,384,1,64]{1,3,2,0:T(8,128)(2,1)} %copy-done.20, f32[]{:T(128)} %bitcast.2, f32[]{:T(128)} %bitcast.3, ...), kind=kLoop, calls=%fused_computation.103 | loop fusion | flops 18874368 | bytes 7194644 | tf_op jit(solution)/shard_map/reduce_sum | solution.py:153
  203.2 27.3 %all_to_all.58 = bf16[1,384,16,64]{1,3,0,2:T(8,128)(2,1)S(1)} all-to-all(bf16[1,384,16,64]{1,3,0,2:T(8,128)(2,1)S(1)} %fusion.80), channel_id=1, replica_groups=mesh['dp'=16,'space'=16] {'space'}, dimensions={2} | all-to-all | bytes 1572864 | tf_op jit(solution)/shard_map/all_to_all | solution.py:71
  230.7 0.9 copy.84
  231.6 2.0 broadcast_in_dim.16
  233.6 3.6 copy.85
  237.2 8.1 %add_convert_fusion = bf16[16,384,2,128]{3,2,1,0:T(2,128)(2,1)} fusion(bf16[16,384,2,128]{3,2,1,0:T(2,128)(2,1)} %param.13, f32[16,384,128]{2,1,0:T(8,128)} %copy.85), kind=kLoop, calls=%fused_computation.61 | loop fusion | flops 4718592 | bytes 9437184 | tf_op jit(solution)/shard_map/convert_element_type | solution.py:162
  245.3 14.1 %fusion.21 = (f32[384]{0:T(512)S(1)}, f32[384]{0:T(512)S(1)}, f32[384]{0:T(512)S(1)}, f32[384]{0:T(512)S(1)}, f32[384]{0:T(512)S(1)}, /*index=5*/f32[384]{0:T(51...) fusion(bf16[16,384,4,130]{1,3,2,0:T(8,128)(2,1)} %copy-done.1, ...), kind=kOutput, calls=%fused_computation.44 | convolution fusion | flops 1256714880 | bytes 31766016 | tf_op jit(solution)/shard_map/cf,bfrw->bcrw/dot_general | solution.py:40
  259.5 2.3 fusion.113
  262.1 3.2 collective-permute-start.2
  265.3 1.3 collective-permute-start.3
  267.3 62.2 %collective-permute-done.2 = bf16[16,384,1,128]{1,3,2,0:T(8,128)(2,1)} collective-permute-done((bf16[16,384,1,128]{1,3,2,0:T(8,128)(2,1)}, bf16[16,384,1,128]{1,3,2,0:T(8,128)(2,1)}, u32[]{:S(2)}, u32[]{:S(2)}) %collective-permute-start.2) | collective-permute-done | bytes 1572896 | tf_op jit(solution)/shard_map/ppermute | solution.py:17
  329.5 5.1 select_maximum_fusion
  334.6 14.0 %fusion.33 = (f32[]{:T(128)}, f32[]{:T(128)}, f32[16,384,128]{1,2,0:T(8,128)S(1)}, f32[16,384,2,128]{1,3,2,0:T(8,128)}) fusion(bf16[16,2,128,384]{3,2,1,0:T(8,128)(2,1)S(1)} %copy-done.22, f32[]{:T(128)S(6)} %add.164, f32[16,384,128]{1,2,0:T(8,128)S(1)} %copy-done.10, f32[]{:T(128)} %bitcast, f32[16,384,128]{1,2,0:T(8,128)S(1)} %copy-done.4, ...), kind=kLoop, calls=%fused_computation.58 | loop fusion | flops 73138176 | bytes 44054032 | tf_op jit(solution)/shard_map/reduce_sum | solution.py:167
  348.6 1.9 bitcast_reduce_fusion
  350.7 1.1 copy.90
  351.7 10.1 %all-to-all-start.4 = ((bf16[16,384,1,64]{1,3,2,0:T(8,128)(2,1)}), bf16[16,384,1,64]{1,3,2,0:T(8,128)(2,1)}, u32[]{:S(2)}, u32[]{:S(2)}) async-start(bf16[16,384,1,64]{1,3,2,0:T(8,128)(2,1)} %copy.90), calls=%async_computation.4 | async-start | bytes 1572864 | tf_op jit(solution)/shard_map/all_to_all | solution.py:67
  364.4 2.7 convolution_bitcast_fusion
  368.0 2.6 fusion.74
  370.7 1.3 fusion.79
  372.0 10.7 %all-to-all-done.4 = bf16[16,384,1,64]{1,3,2,0:T(8,128)(2,1)} async-done(((bf16[16,384,1,64]{1,3,2,0:T(8,128)(2,1)}), bf16[16,384,1,64]{1,3,2,0:T(8,128)(2,1)}, u32[]{:S(2)}, u32[]{:S(2)}) %all-to-all-start.4) | async-done | bytes 786464 | tf_op jit(solution)/shard_map/all_to_all | solution.py:67
  382.6 1.7 convolution_bitcast_fusion.1
  384.4 2.2 fusion.78
  386.6 5.8 fusion.61
  395.4 78.3 %all-reduce.6 = (f32[3,3,384]{2,1,0:T(4,128)}, f32[3,3,384]{2,1,0:T(4,128)}, f32[4]{0:T(128)}) all-reduce(f32[3,3,384]{2,1,0:T(4,128)S(1)} %pad_maximum_fusion.4, f32[3,3,384]{2,1,0:T(4,128)S(1)} %pad_maximum_fusion.5, f32[4]{0:T(128)S(1)} %pad_maximum_fusion.6), channel_id=1, replica_groups=mesh['dp'=16,'space'=16] {'dp','space'}, use_global_device_ids=true, to_apply=%region_17.18 | all-reduce | flops 6916 | bytes 55328 | tf_op jit(solution)/shard_map/psum | solution.py:175
  473.8 172.0 %all-reduce.10.cloned.1.call-done = (f32[80,384]{1,0:T(8,128)}, f32[224,384]{1,0:T(8,128)}, f32[384,384]{1,0:T(8,128)}, f32[384,384]{1,0:T(8,128)}) async-done(((f32[80,384]{1,0:T(8,128)}, f32[224,384]{1,0:T(8,128)}, f32[384,384]{1,0:T(8,128)}, f32[384,384]{1,0:T(8,128)}), (f32[80,384]{1,0:T(8,128)}, f32[224,384]{1,0:T(8,128)}, f32[384,384]{1,0:T(8,128)}, ...) | async-done | bytes 1646608 | tf_op jit(solution)/shard_map/psum | solution.py:175
  645.8 1.6 copy.127
  647.4 1.7 copy.128
  649.1 1.9 copy.129
  651.0 1.9 copy.130
  (108 shorter events, 7.9 us)
Async XLA Ops:
  7.2 168.8 %copy-start = (bf16[1,384,16,64]{1,3,2,0:T(8,128)(2,1)S(1)}, bf16[1,384,16,64]{1,3,2,0:T(8,128)(2,1)}, u32[]{:S(2)}) copy-start(bf16[1,384,16,64]{1,3,2,0:T(8,128)(2,1)} %param.14) | copy-start | bytes 2359300
  7.2 33.8 %copy-start.28 = (f32[4]{0:T(128)S(1)}, f32[4]{0:T(128)}, u32[]{:S(2)}) copy-start(f32[4]{0:T(128)} %param.21) | copy-start | bytes 52
  33.1 0.8 copy-start.11
  36.2 25.3 %all-to-all-start.1 = ((bf16[1,384,16,64]{1,3,0,2:T(8,128)(2,1)}), bf16[1,384,16,64]{1,3,0,2:T(8,128)(2,1)S(1)}, u32[]{:S(2)}, u32[]{:S(2)}) async-start(bf16[1,384,16,64]{1,3,0,2:T(8,128)(2,1)} %bitcast.19), calls=%async_computation.1 | async-start | bytes 1572864 | tf_op jit(solution)/shard_map/all_to_all | solution.py:71
  69.6 2.9 copy-start.23
  69.6 3.0 copy-start.31
  72.6 4.3 copy-start.9
  76.9 74.7 %copy-start.2 = (bf16[16,384,2,128]{1,3,2,0:T(8,128)(2,1)}, bf16[16,384,2,128]{1,3,2,0:T(8,128)(2,1)S(1)}, u32[]{:S(2)}) copy-start(bf16[16,384,2,128]{1,3,2,0:T(8,128)(2,1)S(1)} %get-tuple-element.72) | copy-start | bytes 9437188
  76.9 6.4 copy-start.26
  77.4 34.4 %collective-permute-start.1 = (bf16[16,384,1,128]{1,3,2,0:T(8,128)(2,1)S(1)}, bf16[16,384,1,128]{1,3,2,0:T(8,128)(2,1)S(1)}, u32[]{:S(2)}, u32[]{:S(2)}) collective-permute-start(bf16[16,384,1,128]{1,3,2,0:T(8,128)(2,1)S(1)} %get-tuple-element.65), channel_id=1, source_target_pairs={{1,0},{2,1},{3,2},{4,3},{5,4},{6,5},{7,6},{8,7},{9,8},{10,9},{11,1... | collective-permute-start | bytes 4718600 | tf_op jit(solution)/shard_map/ppermute | solution.py:19
  78.7 69.3 %collective-permute-start = (bf16[16,384,1,128]{1,3,2,0:T(8,128)(2,1)S(1)}, bf16[16,384,1,128]{1,3,2,0:T(8,128)(2,1)S(1)}, u32[]{:S(2)}, u32[]{:S(2)}) collective-permute-start(bf16[16,384,1,128]{1,3,2,0:T(8,128)(2,1)S(1)} %get-tuple-element.66), channel_id=1, source_target_pairs={{0,1},{1,2},{2,3},{3,4},{4,5},{5,6},{6,7},{7,8},{8,9},{9,10},{10,1... | collective-permute-start | bytes 4718600 | tf_op jit(solution)/shard_map/ppermute | solution.py:17
  111.8 39.8 %copy-start.13 = (bf16[16,384,1,128]{1,3,2,0:T(8,128)(2,1)}, bf16[16,384,1,128]{1,3,2,0:T(8,128)(2,1)S(1)}, u32[]{:S(2)}) copy-start(bf16[16,384,1,128]{1,3,2,0:T(8,128)(2,1)S(1)} %collective-permute-done.1) | copy-start | bytes 4718596
  148.0 3.6 copy-start.15
  151.6 7.8 %copy-start.1 = (bf16[16,384,4,130]{1,3,2,0:T(8,128)(2,1)}, bf16[16,384,4,130]{1,3,2,0:T(8,128)(2,1)S(1)}, u32[]{:S(2)}) copy-start(bf16[16,384,4,130]{1,3,2,0:T(8,128)(2,1)S(1)} %fusion.5) | copy-start | bytes 19169284
  151.6 7.8 %copy-start.29 = (bf16[384,384]{1,0:T(8,128)(2,1)S(1)}, bf16[384,384]{1,0:T(8,128)(2,1)}, u32[]{:S(2)}) copy-start(bf16[384,384]{1,0:T(8,128)(2,1)} %param.17) | copy-start | bytes 884740
  159.4 2.1 copy-start.18
  163.5 12.5 %copy-start.25 = (bf16[384,384]{1,0:T(8,128)(2,1)S(1)}, bf16[384,384]{1,0:T(8,128)(2,1)}, u32[]{:S(2)}) copy-start(bf16[384,384]{1,0:T(8,128)(2,1)} %param.18) | copy-start | bytes 884740
  164.9 12.8 %copy-start.27 = (f32[3,3,384]{2,1,0:T(4,128)S(1)}, f32[3,3,384]{2,1,0:T(4,128)}, u32[]{:S(2)}) copy-start(f32[3,3,384]{2,1,0:T(4,128)} %param.20) | copy-start | bytes 41476
  164.9 29.9 %all-to-all-start.2 = ((bf16[16,384,1,64]{1,3,2,0:T(8,128)(2,1)}), bf16[16,384,1,64]{1,3,2,0:T(8,128)(2,1)S(1)}, u32[]{:S(2)}, u32[]{:S(2)}) async-start(bf16[16,384,1,64]{1,3,2,0:T(8,128)(2,1)} %fusion.84), calls=%async_computation.2 | async-start | bytes 1572864 | tf_op jit(solution)/shard_map/all_to_all | solution.py:67
  176.7 0.9 copy-start.7
  194.8 0.9 copy-start.20
  237.2 8.1 %copy-start.3 = (bf16[16,384,2,128]{1,3,2,0:T(8,128)(2,1)S(1)}, bf16[16,384,2,128]{1,3,2,0:T(8,128)(2,1)}, u32[]{:S(2)}) copy-start(bf16[16,384,2,128]{1,3,2,0:T(8,128)(2,1)} %copy-done.2) | copy-start | bytes 9437188
  237.2 8.1 %copy-start.14 = (bf16[16,384,1,128]{1,3,2,0:T(8,128)(2,1)S(1)}, bf16[16,384,1,128]{1,3,2,0:T(8,128)(2,1)}, u32[]{:S(2)}) copy-start(bf16[16,384,1,128]{1,3,2,0:T(8,128)(2,1)} %copy-done.13) | copy-start | bytes 4718596
  237.2 8.1 %copy-start.16 = (bf16[16,384,1,128]{1,3,2,0:T(8,128)(2,1)S(1)}, bf16[16,384,1,128]{1,3,2,0:T(8,128)(2,1)}, u32[]{:S(2)}) copy-start(bf16[16,384,1,128]{1,3,2,0:T(8,128)(2,1)} %copy-done.15) | copy-start | bytes 4718596
  237.2 8.2 %copy-start.30 = (bf16[384,384]{1,0:T(8,128)(2,1)S(1)}, bf16[384,384]{1,0:T(8,128)(2,1)}, u32[]{:S(2)}) copy-start(bf16[384,384]{1,0:T(8,128)(2,1)} %param.17) | copy-start | bytes 884740
  259.5 2.6 copy-start.5
  262.1 67.3 %collective-permute-start.2 = (bf16[16,384,1,128]{1,3,2,0:T(8,128)(2,1)}, bf16[16,384,1,128]{1,3,2,0:T(8,128)(2,1)}, u32[]{:S(2)}, u32[]{:S(2)}) collective-permute-start(bf16[16,384,1,128]{1,3,2,0:T(8,128)(2,1)} %get-tuple-element.63), channel_id=1, source_target_pairs={{0,1},{1,2},{2,3},{3,4},{4,5},{5,6},{6,7},{7,8},{8,9},{9,10},{10,1... | collective-permute-start | bytes 4718600 | tf_op jit(solution)/shard_map/ppermute | solution.py:17
  265.3 64.1 %collective-permute-start.3 = (bf16[16,384,1,128]{1,3,2,0:T(8,128)(2,1)}, bf16[16,384,1,128]{1,3,2,0:T(8,128)(2,1)}, u32[]{:S(2)}, u32[]{:S(2)}) collective-permute-start(bf16[16,384,1,128]{1,3,2,0:T(8,128)(2,1)} %get-tuple-element.64), channel_id=1, source_target_pairs={{1,0},{2,1},{3,2},{4,3},{5,4},{6,5},{7,6},{8,7},{9,8},{10,9},{11,1... | collective-permute-start | bytes 4718600 | tf_op jit(solution)/shard_map/ppermute | solution.py:19
  267.3 67.3 %copy-start.4 = (f32[16,384,128]{1,2,0:T(8,128)S(1)}, f32[16,384,128]{1,2,0:T(8,128)}, u32[]{:S(2)}) copy-start(f32[16,384,128]{1,2,0:T(8,128)} %convert_element_type.335) | copy-start | bytes 9437188
  267.3 67.3 %copy-start.6 = (bf16[16,384,2,128]{1,3,2,0:T(8,128)(2,1)S(1)}, bf16[16,384,2,128]{1,3,2,0:T(8,128)(2,1)}, u32[]{:S(2)}) copy-start(bf16[16,384,2,128]{1,3,2,0:T(8,128)(2,1)} %copy-done.5) | copy-start | bytes 9437188
  267.3 67.3 %copy-start.10 = (f32[16,384,128]{1,2,0:T(8,128)S(1)}, f32[16,384,128]{1,2,0:T(8,128)}, u32[]{:S(2)}) copy-start(f32[16,384,128]{1,2,0:T(8,128)} %copy-done.9) | copy-start | bytes 9437188
  267.3 67.3 %copy-start.22 = (bf16[16,2,128,384]{3,2,1,0:T(8,128)(2,1)S(1)}, bf16[16,2,128,384]{3,2,1,0:T(8,128)(2,1)}, u32[]{:S(2)}) copy-start(bf16[16,2,128,384]{3,2,1,0:T(8,128)(2,1)} %get-tuple-element.73) | copy-start | bytes 9437188
  350.5 12.8 %copy-start.12 = (bf16[1,384,16,64]{1,3,2,0:T(8,128)(2,1)S(1)}, bf16[1,384,16,64]{1,3,2,0:T(8,128)(2,1)}, u32[]{:S(2)}) copy-start(bf16[1,384,16,64]{1,3,2,0:T(8,128)(2,1)} %get-tuple-element.67) | copy-start | bytes 2359300
  351.7 30.9 %all-to-all-start.4 = ((bf16[16,384,1,64]{1,3,2,0:T(8,128)(2,1)}), bf16[16,384,1,64]{1,3,2,0:T(8,128)(2,1)}, u32[]{:S(2)}, u32[]{:S(2)}) async-start(bf16[16,384,1,64]{1,3,2,0:T(8,128)(2,1)} %copy.90), calls=%async_computation.4 | async-start | bytes 1572864 | tf_op jit(solution)/shard_map/all_to_all | solution.py:67
  361.8 284.0 %all-reduce.10.cloned.1.call-start = ((), (), s32[]{:S(2)}) async-start(), calls=%async_computation.5 | async-start | bytes 3293184 | tf_op jit(solution)/shard_map/psum | solution.py:175
  363.4 7.3 %slice-start = ((s8[6291456]{0:T(1024)(128)(4,1)}), s8[4194304]{0:T(1024)(128)(4,1)S(1)}, s32[]{:S(2)}) async-start(s8[6291456]{0:T(1024)(128)(4,1)} %bitcast.201), calls=%async_computation.6 | async-start | bytes 8388608
  363.5 0.9 copy-start.17
  364.4 2.7 copy-start.19
  364.4 3.6 copy-start.21
  364.4 6.2 slice-start.1
  368.0 2.7 copy-start.24
  372.0 14.7 %copy-start.8 = (bf16[1,384,16,64]{1,3,2,0:T(8,128)(2,1)S(1)}, bf16[1,384,16,64]{1,3,2,0:T(8,128)(2,1)}, u32[]{:S(2)}) copy-start(bf16[1,384,16,64]{1,3,2,0:T(8,128)(2,1)} %copy-done.7) | copy-start | bytes 2359300
Sparse Core Ops, SparseCore 0:
  386.7 259.0 all-reduce.9
where the time goes:
time: 667 us; the launch traced here: 660 us
  waiting for transfers between devices  345 us (52%)
  blocking collectives  132 us (20%)
  other arithmetic  60.6 us (9%)
  starting transfers between devices  34.5 us (5%)
  matrix products  34 us (5%)
  local copies, waits for them, and re-layouts  31.3 us (5%)
  between operations  22.8 us (3%)
    psum x1, waiting for transfers between devices, body(): lax.psum((lateral_fine_grad, lateral_coarse_grad, point_fine_grad, point_...  172 us
    ppermute x2, waiting for transfers between devices, extended(): lax.ppermute(tail, axis, [(i, (i + 1) % count) for i in range(ends)])  98.4 us
    psum x1, blocking collectives, body(): lax.psum((lateral_fine_grad, lateral_coarse_grad, point_fine_grad, point_...  78.3 us
    ppermute x2, waiting for transfers between devices, extended(): lax.ppermute(head, axis, [((i + 1) % count, i) for i in range(ends)])  28.5 us
    all_to_all x2, waiting for transfers between devices, to_batch(): lax.all_to_all(values, 'space', split_axis=0, concat_axis=2, tiled=True)  27.7 us
    all_to_all x1, blocking collectives, to_rows(): lax.all_to_all(values, 'space', split_axis=2, concat_axis=0, tiled=True)  27.3 us
    all_to_all x1, blocking collectives, to_batch(): lax.all_to_all(values, 'space', split_axis=0, concat_axis=2, tiled=True)  25.9 us
    all_to_all x2, starting transfers between devices, to_batch(): lax.all_to_all(values, 'space', split_axis=0, concat_axis=2, tiled=True)  19.2 us
  transfers between devices with their start and end apart: 8, of which 7 were waited for; matrix products, arithmetic and copies ran while one was open for 2% of the time, Pallas kernels for 0%

commit v1 on v0

v1 whole, which is shorter than its diff:
```python
import jax
import jax.numpy as jnp
import numpy as np
from jax import lax
from jax.experimental import pallas as pl
from jax.experimental.pallas import tpu as pltpu
from jax.sharding import PartitionSpec as P

EPSILON = 0.0001
F = 384
FB = 128
CH = 16
ROWS = 32
PAIRS = 8
HALF = jnp.bfloat16
WIDE = jnp.float32
ALL = ("dp", "space")
LIMIT = 50 * 1024 * 1024


def nn(left, right):
    return lax.dot_general(left, right, (((1,), (0,)), ((), ())), preferred_element_type=WIDE)


def nt(left, right):
    return lax.dot_general(left, right, (((1,), (1,)), ((), ())), preferred_element_type=WIDE)


def upsampler():
    out = np.zeros((128, 256), np.float32)
    for col in range(128):
        out[col, 2 * col] = 1.0
        out[col, 2 * col + 1] = 1.0
    return out


def upsampler_rows():
    one = upsampler()
    out = np.zeros((2, 128, 256), np.float32)
    for odd in range(2):
        half = one[:, 128 * odd : 128 * odd + 128]
        out[odd, :, :128] = half
        out[odd, :, 128:] = half
    return out


def pooler(scale):
    one = upsampler()
    out = np.zeros((512, 128), np.float32)
    for row in range(4):
        out[128 * row : 128 * row + 128] = one[:, 128 * (row // 2) : 128 * (row // 2) + 128].T
    return out * scale


def lanes(shape):
    return lax.broadcasted_iota(jnp.int32, shape, 1)


def side_fine(cells, lane):
    before = jnp.where(lane == 0, 0.0, pltpu.roll(cells, 1, 1))
    after = jnp.where(lane == 127, 0.0, pltpu.roll(cells, 127, 1))
    return before, cells, after


def side_coarse(cells, lane):
    before = jnp.where((lane % 64) == 0, 0.0, pltpu.roll(cells, 1, 1))
    after = jnp.where((lane % 64) == 63, 0.0, pltpu.roll(cells, 127, 1))
    return before, cells, after


def taps_of(ref, start):
    return [
        [
            jnp.broadcast_to(ref[pl.ds(start, CH), 3 * u + v : 3 * u + v + 1], (CH, 128))
            for v in range(3)
        ]
        for u in range(3)
    ]


def lane_sum(values):
    return jnp.sum(values, axis=1, keepdims=True)


def sigmoid(values):
    return 1.0 / (1.0 + jnp.exp(-values))


def forward_kernel(
    coef, fine, coarse, lat_fine, lat_coarse, kern, up, pool,
    act_out, slope_out, depth_out, proj_out, pooled_out, proj, lifted,
):
    lifted_low = nt(lat_coarse[...], coarse[...]).astype(HALF)
    for k in range(PAIRS):
        pair = lifted_low[:, 128 * k : 128 * k + 128]
        proj_out[k] = pair
        both = nn(pair, up[...])
        lifted[2 * k] = both[:, :128]
        lifted[2 * k + 1] = both[:, 128:]
    for s in range(ROWS // 2):
        both = nn(lat_fine[...], jnp.concatenate([fine[2 * s], fine[2 * s + 1]], axis=1))
        proj[2 * s] = both[:, :128]
        proj[2 * s + 1] = both[:, 128:]
    own, above = coef[0], coef[1]

    @pl.loop(0, FB // CH)
    def _(step):
        start = pl.multiple_of(step * CH, CH)
        at = pl.ds(start, CH)
        taps = taps_of(kern, start)
        lane = lanes((CH, 128))
        sides = {}
        for r in range(ROWS + 1):
            if r < ROWS:
                joined = own * proj[r, at, :] + above * lifted[r // 2, at, :]
                gate = sigmoid(joined)
                active = joined * gate
                act_out[r, at, :] = active.astype(HALF)
                slope_out[r, at, :] = (gate * (1.0 + joined * (1.0 - gate))).astype(HALF)
                sides[r] = side_fine(active, lane)
            if r >= 1:
                total = None
                for u in range(3):
                    if r - 2 + u not in sides:
                        continue
                    for v in range(3):
                        term = taps[u][v] * sides[r - 2 + u][v]
                        total = term if total is None else total + term
                depth_out[r - 1, at, :] = total.astype(HALF)
                sides.pop(r - 2, None)

    for k in range(PAIRS):
        four = jnp.concatenate([depth_out[4 * k + a] for a in range(4)], axis=1)
        pooled_out[k] = nn(four, pool[...]).astype(HALF)


def coarse_kernel(
    coef, pooled_depth, proj, point_fine, point_fine_t, point_coarse, cotan, coarse, kern,
    grad_point, grad_kern, grad_point_fine, quarter_back, grad_lat, sums,
    pooled, active_s, gate_s, back_s, depth_s, pooled_back, own_back,
):
    own, down, scale_own, scale_down = coef[2], coef[3], coef[4], coef[5]
    for k in range(PAIRS):
        pooled[k] = nn(point_fine_t[...], pooled_depth[k]).astype(HALF).astype(WIDE)
        back_s[k] = nt(point_coarse[...], cotan[k]).astype(HALF).astype(WIDE)
    sums[...] = jnp.zeros_like(sums)

    def rows_of(cells, lane):
        turned = [pltpu.roll(c, 64, 1) for c in cells]
        low = lane < 64
        nil = jnp.zeros((CH, 128), WIDE)
        out = []
        for k in range(PAIRS):
            above = jnp.where(low, turned[k - 1] if k else nil, turned[k])
            below = jnp.where(low, turned[k], turned[k + 1] if k + 1 < PAIRS else nil)
            out.append([side_coarse(c, lane) for c in (above, cells[k], below)])
        return out

    @pl.loop(0, F // CH)
    def _(step):
        start = pl.multiple_of(step * CH, CH)
        at = pl.ds(start, CH)
        taps = taps_of(kern, start)
        lane = lanes((CH, 128))
        active, steep = [], []
        for k in range(PAIRS):
            joined = own * proj[k, at, :].astype(WIDE) + down * pooled[k, at, :]
            gate = sigmoid(joined)
            active.append(joined * gate)
            gate_s[k, at, :] = gate * (1.0 + joined * (1.0 - gate))
        near = rows_of(active, lane)
        for k in range(PAIRS):
            active_s[k, at, :] = active[k]
            total = None
            for u in range(3):
                for v in range(3):
                    term = taps[u][v] * near[k][u][v]
                    total = term if total is None else total + term
            depth_s[k, at, :] = total.astype(HALF)

    @pl.loop(0, F // CH)
    def _(step):
        start = pl.multiple_of(step * CH, CH)
        at = pl.ds(start, CH)
        taps = taps_of(kern, start)
        lane = lanes((CH, 128))
        near = rows_of([back_s[k, at, :] for k in range(PAIRS)], lane)
        weight = [[jnp.zeros((CH, 128), WIDE) for _ in range(3)] for _ in range(3)]
        sum_own = jnp.zeros((CH, 128), WIDE)
        sum_down = jnp.zeros((CH, 128), WIDE)
        for k in range(PAIRS):
            active = active_s[k, at, :]
            total = None
            for u in range(3):
                for v in range(3):
                    shifted = near[k][2 - u][2 - v]
                    term = taps[u][v] * shifted
                    total = term if total is None else total + term
                    weight[u][v] = weight[u][v] + shifted * active
            slope = total * gate_s[k, at, :]
            sum_own = sum_own + slope * proj[k, at, :].astype(WIDE)
            sum_down = sum_down + slope * pooled[k, at, :]
            pooled_back[k, at, :] = (scale_down * slope).astype(HALF)
            own_back[k, at, :] = (scale_own * slope).astype(HALF)
        for u in range(3):
            for v in range(3):
                grad_kern[at, 3 * u + v : 3 * u + v + 1] = lane_sum(weight[u][v])
        sums[0] += sum_own
        sums[1] += sum_down

    def accumulate(total, term):
        return term if total is None else total + term

    point, point_f, lat = None, None, None
    for k in range(PAIRS):
        point = accumulate(point, nn(depth_s[k], cotan[k]))
        point_f = accumulate(point_f, nt(pooled_depth[k], pooled_back[k]))
        lat = accumulate(lat, nn(own_back[k], coarse[k]))
        quarter_back[k] = (0.25 * nn(point_fine[...], pooled_back[k])).astype(HALF)
    grad_point[...] = point
    grad_point_fine[...] = point_f
    grad_lat[...] = lat


def backward_kernel(
    coef, cotan, point, quarter_back, act, steep, depth, fine, coarse, lat_fine, lat_coarse,
    kern, up, pool, part_point, part_lat,
    grad_point, grad_lat_fine, grad_lat_coarse, grad_kern, sums,
    back, slope_s,
):
    for s in range(ROWS // 2):
        both = nn(
            jnp.concatenate([point[...], quarter_back[s // 2]], axis=1),
            jnp.concatenate(
                [jnp.concatenate([cotan[2 * s], cotan[2 * s + 1]], axis=1), up[s % 2]], axis=0
            ),
        )
        back[2 * s] = both[:, :128]
        back[2 * s + 1] = both[:, 128:]

    @pl.loop(0, FB // CH)
    def _(step):
        start = pl.multiple_of(step * CH, CH)
        at = pl.ds(start, CH)
        taps = taps_of(kern, start)
        lane = lanes((CH, 128))
        weight = [[None] * 3 for _ in range(3)]
        sides = {}
        for r in range(ROWS + 1):
            if r < ROWS:
                sides[r] = side_fine(back[r, at, :], lane)
            if r >= 1:
                active = act[r - 1, at, :].astype(WIDE)
                total = None
                for u in range(3):
                    if r - u not in sides:
                        continue
                    for v in range(3):
                        shifted = sides[r - u][2 - v]
                        term = taps[u][v] * shifted
                        total = term if total is None else total + term
                        more = active * shifted
                        weight[u][v] = more if weight[u][v] is None else weight[u][v] + more
                slope_s[r - 1, at, :] = (total * steep[r - 1, at, :].astype(WIDE)).astype(HALF)
                sides.pop(r - 2, None)
        for u in range(3):
            for v in range(3):
                grad_kern[at, 3 * u + v : 3 * u + v + 1] = lane_sum(weight[u][v])

    def accumulate(total, term):
        return term if total is None else total + term

    point_g, lat_f, lat_c = None, None, None
    for k in range(PAIRS):
        pooled = []
        for a in range(2):
            s = 2 * k + a
            two = jnp.concatenate([slope_s[2 * s], slope_s[2 * s + 1]], axis=1)
            lat_f = accumulate(
                lat_f, nt(two, jnp.concatenate([fine[2 * s], fine[2 * s + 1]], axis=1))
            )
            point_g = accumulate(
                point_g,
                nt(
                    jnp.concatenate([depth[2 * s], depth[2 * s + 1]], axis=1),
                    jnp.concatenate([cotan[2 * s], cotan[2 * s + 1]], axis=1),
                ),
            )
            pooled.append(two)
        lat_c = accumulate(
            lat_c, nn(nn(jnp.concatenate(pooled, axis=1), pool[...]).astype(HALF), coarse[k])
        )
    grad_point[...] = point_g + part_point[...]
    grad_lat_fine[...] = coef[6] * lat_f
    grad_lat_coarse[...] = coef[7] * lat_c + part_lat[...]
    first = jnp.sum(lat_f * lat_fine[...].astype(WIDE), axis=0, keepdims=True)
    second = jnp.sum(lat_c * lat_coarse[...].astype(WIDE), axis=0, keepdims=True)
    row = lax.broadcasted_iota(jnp.int32, (8, 128), 0)
    sums[0] = jnp.where(row == 0, jnp.sum(first), jnp.where(row == 1, jnp.sum(second), 0.0))


def shaped(*shape, dtype=WIDE):
    return jax.ShapeDtypeStruct(shape, dtype)


def params(kind=None):
    return pltpu.CompilerParams(vmem_limit_bytes=LIMIT, dimension_semantics=kind)


SMEM = pl.BlockSpec(memory_space=pltpu.SMEM)


def whole(*shape):
    return pl.BlockSpec(shape, lambda j: (0,) * len(shape))


def rows_at(count):
    return pl.BlockSpec((count, FB, 128), lambda j: (0, j, 0))


def cols_at(width):
    return pl.BlockSpec((FB, width), lambda j: (j, 0))


def forward(coef, fine, coarse, lat_fine, lat_coarse, kern):
    return pl.pallas_call(
        forward_kernel,
        name="forward",
        grid=(F // FB,),
        in_specs=[
            SMEM, whole(ROWS, 80, 128), whole(1024, 224), cols_at(80), cols_at(224), cols_at(9),
            whole(128, 256), whole(512, 128),
        ],
        out_specs=[rows_at(ROWS), rows_at(ROWS), rows_at(ROWS), rows_at(PAIRS), rows_at(PAIRS)],
        out_shape=[shaped(ROWS, F, 128, dtype=HALF)] * 3 + [shaped(PAIRS, F, 128, dtype=HALF)] * 2,
        scratch_shapes=[
            pltpu.VMEM((ROWS, FB, 128), WIDE),
            pltpu.VMEM((ROWS // 2, FB, 128), WIDE),
        ],
        compiler_params=params(("arbitrary",)),
        cost_estimate=pl.CostEstimate(flops=10**9, bytes_accessed=12 * 10**6, transcendentals=10**6),
    )(
        coef, fine, coarse, lat_fine, lat_coarse, kern,
        jnp.asarray(upsampler(), HALF), jnp.asarray(pooler(0.25), HALF),
    )


def coarse_node(coef, pooled_depth, proj, point_fine, point_coarse, cotan, coarse, kern):
    return pl.pallas_call(
        coarse_kernel,
        name="coarse_node",
        in_specs=[SMEM] + [pl.BlockSpec(memory_space=pltpu.VMEM)] * 8,
        out_specs=[pl.BlockSpec(memory_space=pltpu.VMEM)] * 6,
        out_shape=[
            shaped(F, F), shaped(F, 9), shaped(F, F), shaped(PAIRS, F, 128, dtype=HALF),
            shaped(F, 224), shaped(2, CH, 128),
        ],
        scratch_shapes=[pltpu.VMEM((PAIRS, F, 128), WIDE)] * 4
        + [pltpu.VMEM((PAIRS, F, 128), HALF)] * 3,
        compiler_params=params(),
        cost_estimate=pl.CostEstimate(flops=10**9, bytes_accessed=5 * 10**6, transcendentals=10**6),
    )(
        coef, pooled_depth, proj, point_fine, point_fine.T, point_coarse,
        cotan.reshape(PAIRS, 128, F), coarse.reshape(PAIRS, 128, 224), kern,
    )


def backward(
    coef, cotan, point, quarter_back, act, steep, depth, fine, coarse, lat_fine, lat_coarse,
    kern, part_point, part_lat,
):
    return pl.pallas_call(
        backward_kernel,
        name="backward",
        grid=(F // FB,),
        in_specs=[
            SMEM, whole(ROWS, F, 128), cols_at(F), rows_at(PAIRS), rows_at(ROWS), rows_at(ROWS),
            rows_at(ROWS), whole(ROWS, 80, 128), whole(PAIRS, 128, 224), cols_at(80),
            cols_at(224), cols_at(9), whole(2, 128, 256), whole(512, 128), cols_at(F),
            cols_at(224),
        ],
        out_specs=[
            cols_at(F), cols_at(80), cols_at(224), cols_at(9),
            pl.BlockSpec((1, 8, 128), lambda j: (j, 0, 0)),
        ],
        out_shape=[shaped(F, F), shaped(F, 80), shaped(F, 224), shaped(F, 9), shaped(F // FB, 8, 128)],
        scratch_shapes=[
            pltpu.VMEM((ROWS, FB, 128), WIDE),
            pltpu.VMEM((ROWS, FB, 128), HALF),
        ],
        compiler_params=params(("arbitrary",)),
        cost_estimate=pl.CostEstimate(flops=3 * 10**9, bytes_accessed=16 * 10**6, transcendentals=0),
    )(
        coef, cotan, point, quarter_back, act, steep, depth, fine,
        coarse.reshape(PAIRS, 128, 224), lat_fine, lat_coarse, kern,
        jnp.asarray(upsampler_rows(), HALF), jnp.asarray(pooler(1.0), HALF), part_point, part_lat,
    )


def to_images(values):
    return lax.all_to_all(values, "space", split_axis=0, concat_axis=0, tiled=True)


def thirds(values):
    high = values.astype(HALF)
    rest = values - high.astype(WIDE)
    middle = rest.astype(HALF)
    return jnp.concatenate([high, middle, (rest - middle.astype(WIDE)).astype(HALF)])


def total_over_devices(parts):
    flat = jnp.concatenate([p.astype(HALF).reshape(-1) for p in parts])
    count = lax.axis_size("dp") * lax.axis_size("space")
    share = -(-flat.size // (count * 128)) * 128
    flat = jnp.pad(flat, (0, count * share - flat.size)).reshape(count, share // 128, 128)
    mine = lax.all_to_all(flat, ALL, split_axis=0, concat_axis=0, tiled=True)
    mine = jnp.sum(mine.astype(WIDE), axis=0).astype(HALF)
    mine = jnp.broadcast_to(mine[None], (count,) + mine.shape)
    mine = lax.optimization_barrier(mine)
    full = lax.all_to_all(mine, ALL, split_axis=0, concat_axis=0, tiled=True).reshape(-1)
    out, start = [], 0
    for p in parts:
        out.append(full[start : start + p.size].reshape(p.shape).astype(WIDE))
        start += p.size
    return out


def body(
    fine_map,
    coarse_map,
    fine_cotan,
    coarse_cotan,
    lateral_fine,
    lateral_coarse,
    point_fine,
    point_coarse,
    kernel_fine,
    kernel_coarse,
    joining,
):
    fine_total = joining[0] + joining[1] + EPSILON
    coarse_total = joining[2] + joining[3] + EPSILON
    ratio = joining / jnp.stack([fine_total, fine_total, coarse_total, coarse_total])
    coef = jnp.concatenate([ratio, ratio[2:], ratio[:2]])
    coarse = to_images(jnp.transpose(coarse_map, (0, 2, 3, 1)).reshape(16, 64, 224))
    fine = to_images(jnp.transpose(fine_map, (0, 2, 1, 3))).reshape(ROWS, 80, 128)
    cotan = to_images(jnp.transpose(fine_cotan, (0, 2, 1, 3))).reshape(ROWS, F, 128)
    coarse_cot = jnp.transpose(coarse_cotan, (0, 2, 3, 1)).reshape(1024, F)
    coarse = coarse.reshape(1024, 224)
    lat_fine, lat_coarse = lateral_fine.T, lateral_coarse.T
    kern_fine = kernel_fine.reshape(9, F).T
    kern_coarse = kernel_coarse.reshape(9, F).T
    act, steep, depth, proj_coarse, pooled_depth = forward(
        coef, fine, coarse, lat_fine, lat_coarse, kern_fine
    )
    grad_point_coarse, grad_kern_coarse, part_point, quarter_back, part_lat, sums_coarse = (
        coarse_node(
            coef, pooled_depth, proj_coarse, point_fine, point_coarse, coarse_cot, coarse,
            kern_coarse,
        )
    )
    grad_point_fine, grad_lat_fine, grad_lat_coarse, grad_kern_fine, sums_fine = backward(
        coef, cotan, point_fine, quarter_back, act, steep, depth, fine, coarse, lat_fine,
        lat_coarse, kern_fine, part_point, part_lat,
    )
    sums = jnp.concatenate([sums_fine[:, :2, 0].sum(axis=0), sums_coarse.sum(axis=(1, 2))])
    mean_fine = ratio[0] * sums[0] + ratio[1] * sums[1]
    mean_coarse = ratio[2] * sums[2] + ratio[3] * sums[3]
    join_term = jnp.concatenate(
        [(sums[:2] - mean_fine) / fine_total, (sums[2:] - mean_coarse) / coarse_total]
    )
    early = total_over_devices([grad_point_coarse, grad_kern_coarse])
    late = total_over_devices(
        [grad_point_fine, grad_lat_fine, grad_lat_coarse, grad_kern_fine, thirds(join_term)]
    )
    grad_joining = late[4].reshape(3, 4).sum(axis=0)
    return (
        late[1].T,
        late[2].T,
        late[0],
        early[0],
        late[3].T.reshape(3, 3, F),
        early[1].T.reshape(3, 3, F),
        grad_joining,
    )


def solution(mesh):
    return jax.shard_map(
        body,
        mesh=mesh,
        in_specs=(
            P("dp", None, "space", None),
            P("dp", None, "space", None),
            P("dp", None, "space", None),
            P(("dp", "space"), None, None, None),
            P(),
            P(),
            P(),
            P(),
            P(),
            P(),
            P(),
        ),
        out_specs=(P(), P(), P(), P(), P(), P(), P()),
        check_vma=False,
    )
```

time: 667 us -> 376 us (0.56)
  waiting for transfers between devices: 345 us -> 135 us
  blocking collectives: 132 us -> 63 us
  other arithmetic: 60.6 us -> 3.44 us
  Pallas kernels: 0 us -> 56.7 us
  local copies, waits for them, and re-layouts: 31.3 us -> 69.3 us
  matrix products: 34 us -> 0 us
  between operations: 22.8 us -> 8.76 us
    psum x1 -> x0, waiting for transfers between devices: 172 us -> none  [body(): lax.psum((lateral_fine_grad, lateral_coarse_grad, point_fine_grad, point_...]
    ppermute x4 -> x0, waiting for transfers between devices: 127 us -> none  [the longest x2 98.4 us: extended(): lax.ppermute(tail, axis, [(i, (i + 1) % count) for i in range(ends)])]
    all_to_all x3 -> x5, waiting for transfers between devices: 46.3 us -> 135 us  [the longest x2 74.8 us: to_images(): lax.all_to_all(values, 'space', split_axis=0, concat_axis=0, tiled=True)]
    psum x1 -> x0, blocking collectives: 78.3 us -> none  [body(): lax.psum((lateral_fine_grad, lateral_coarse_grad, point_fine_grad, point_...]
    pallas_call x0 -> x3, Pallas kernels: none -> 56.7 us  [the longest x1 24.2 us: backward(): pl.pallas_call(backward_kernel, name='backward', grid=(F // FB,), in_spec...]
    slice x5, local copies, waits for them, and re-layouts: 3.49 us -> 44.7 us  [the longest x1 42 us: total_over_devices(): out.append(full[start:start + p.size].reshape(p.shape).astype(WIDE))]
    dot_general x10 -> x0, matrix products: 34 us -> none  [the longest x2 14.8 us: project_back(): jnp.einsum('cf,bfrw->bcrw', weight, cotangent, preferred_element_type=jnp...]
    reduce_sum x5, other arithmetic: 31.2 us -> 1.95 us  [the longest x1 1.18 us: body(): grad_joining = late[4].reshape(3, 4).sum(axis=0)]
  transfers between devices with their start and end apart: 8 -> 5, of which waited for: 7 -> 4; matrix products, arithmetic and copies ran while one was open for 2% -> 5% of each run, Pallas kernels for 0% -> 6%
where the time goes in v1:
time: 376 us; the launch traced here: 375 us
  waiting for transfers between devices  135 us (36%)
  local copies, waits for them, and re-layouts  69.3 us (18%)
  blocking collectives  63 us (17%)
  Pallas kernels  56.7 us (15%)
  starting transfers between devices  38.7 us (10%)
  between operations  8.76 us (2%)
    all_to_all x2, waiting for transfers between devices, to_images(): lax.all_to_all(values, 'space', split_axis=0, concat_axis=0, tiled=True)  74.8 us
    slice x1, local copies, waits for them, and re-layouts, total_over_devices(): out.append(full[start:start + p.size].reshape(p.shape).astype(WIDE))  42 us
    all_to_all x1, blocking collectives, total_over_devices(): mine = lax.all_to_all(flat, ALL, split_axis=0, concat_axis=0, tiled=True)  33.1 us
    all_to_all x1, waiting for transfers between devices, total_over_devices(): mine = lax.all_to_all(flat, ALL, split_axis=0, concat_axis=0, tiled=True)  30.5 us
    all_to_all x1, blocking collectives, to_images(): lax.all_to_all(values, 'space', split_axis=0, concat_axis=0, tiled=True)  29.8 us
    all_to_all x2, waiting for transfers between devices, total_over_devices(): lax.all_to_all(mine, ALL, split_axis=0, concat_axis=0, tiled=True)  29.7 us
    pallas_call x1, Pallas kernels, backward(): pl.pallas_call(backward_kernel, name='backward', grid=(F // FB,), in_spec...  24.2 us
    pallas_call x1, Pallas kernels, coarse_node(): pl.pallas_call(coarse_kernel, name='coarse_node', in_specs=[SMEM] + [pl.B...  19.5 us
  transfers between devices with their start and end apart: 5, of which 4 were waited for; matrix products, arithmetic and copies ran while one was open for 5% of the time, Pallas kernels for 6%

profile of v1, /device:TPU:1, one launch (start us, length us, event | category | flops | bytes accessed | tf_op | source)
XLA Modules:
  0.0 374.8 jit_solution(1776318997928050099)
XLA Ops:
  0.7 29.8 %all_to_all.35 = bf16[16,2,80,128]{3,1,2,0:T(2,128)(2,1)S(1)} all-to-all(bf16[16,2,80,128]{3,1,2,0:T(2,128)(2,1)} %bitcast.45), channel_id=1, replica_groups=mesh['dp'=16,'space'=16] {'space'}, dimensions={0} | all-to-all | bytes 1310720 | tf_op jit(solution)/shard_map/all_to_all | solution.py:401
  30.5 3.6 all-to-all-start.2
  34.1 1.4 fusion.8
  38.1 0.7 reshape.117
  39.0 1.1 copy.43
  40.1 0.9 copy.42
  41.0 0.2 copy.45
  41.8 6.6 %all-to-all-done.2 = bf16[16,64,224]{2,1,0:T(8,128)(2,1)S(1)} async-done(((bf16[16,64,224]{2,1,0:T(8,128)(2,1)}), bf16[16,64,224]{2,1,0:T(8,128)(2,1)S(1)}, u32[]{:S(2)}, u32[]{:S(2)}) %all-to-all-start.2) | async-done | bytes 458784 | tf_op jit(solution)/shard_map/all_to_all | solution.py:401
  48.4 12.9 %forward.1 = (bf16[32,384,128]{2,1,0:T(8,128)(2,1)}, bf16[32,384,128]{2,1,0:T(8,128)(2,1)}, bf16[32,384,128]{2,1,0:T(8,128)(2,1)}, bf16[8,384,128]{2,1,0:T(8,128)(2,1)S(1)}, bf16[8,384,128]{2,1,0:T(8,128)(2,1)S(1)}) custom-call(f32[8]{0:T(128)S(1)} %pad_maximum_fusion.coef, bf16[32,80,128]{2,1,0:T(8,128)(2,1)S(1)} %bitcast.28, ...), custom_call_target="tpu_custom_call" | custom-call | flops 1000000000 | bytes 12000000 | tf_op jit(solution)/shard_map/forward/pallas_call | solution.py:326
  61.3 0.9 copy-done.2
  62.2 0.9 copy-done.3
  63.1 1.0 copy-done.4
  64.1 19.5 %coarse_node.1 = (f32[384,384]{1,0:T(8,128)S(1)}, f32[384,9]{1,0:T(8,128)S(1)}, f32[384,384]{1,0:T(8,128)S(1)}, bf16[8,384,128]{2,1,0:T(8,128)(2,1)}, f32[384,224]{1,0:T(8,128)S(1)}, /*index=5*/f32[2,16,128]{2,1,0:T(8,128)S(1)}) custom-call(f32[8]{0:T(128)S(1)} %pad_maximum_fusion.coef, bf16[8,384,128]{2,1,0:T(8,128)(2,1)} %copy-done.3, ...), custom_call_target="tpu_custom_call" | custom-call | flops 1000000000 | bytes 5000000 | tf_op jit(solution)/shard_map/coarse_node/pallas_call | solution.py:349
  83.6 0.7 copy-done.5
  84.4 0.9 convert_element_type.87
  85.4 0.2 reshape.126
  85.8 33.1 %all_to_all.36 = bf16[256,5,128]{2,1,0:T(8,128)(2,1)S(1)} all-to-all(bf16[256,5,128]{2,1,0:T(8,128)(2,1)S(1)} %reshape.127), channel_id=1, replica_groups=mesh['dp'=16,'space'=16] {'dp','space'}, dimensions={0} | all-to-all | bytes 655360 | tf_op jit(solution)/shard_map/all_to_all | solution.py:416
  118.9 4.5 %all-to-all-start = ((bf16[16,2,384,128]{3,1,2,0:T(2,128)(2,1)}), bf16[16,2,384,128]{3,1,2,0:T(2,128)(2,1)}, u32[]{:S(2)}, u32[]{:S(2)}) async-start(bf16[16,2,384,128]{3,1,2,0:T(2,128)(2,1)} %bitcast.39), calls=%async_computation | async-start | bytes 6291456 | tf_op jit(solution)/shard_map/all_to_all | solution.py:401
  123.5 0.7 fusion.5
  126.7 0.3 reduce_sum.54
  127.0 0.9 broadcast_in_dim.5
  127.9 68.2 %all-to-all-done = bf16[16,2,384,128]{3,1,2,0:T(2,128)(2,1)} async-done(((bf16[16,2,384,128]{3,1,2,0:T(2,128)(2,1)}), bf16[16,2,384,128]{3,1,2,0:T(2,128)(2,1)}, u32[]{:S(2)}, u32[]{:S(2)}) %all-to-all-start) | async-done | bytes 3145760 | tf_op jit(solution)/shard_map/all_to_all | solution.py:401
  196.1 11.2 %all-to-all-start.6 = ((bf16[256,5,128]{2,1,0:T(8,128)(2,1)}), bf16[256,5,128]{2,1,0:T(8,128)(2,1)}, u32[]{:S(2)}, u32[]{:S(2)}) async-start(bf16[256,5,128]{2,1,0:T(8,128)(2,1)} %broadcast_in_dim.5), calls=%async_computation.6 | async-start | bytes 1048576 | tf_op jit(solution)/shard_map/all_to_all | solution.py:420
  207.3 4.4 %copy.40 = bf16[16,2,384,128]{3,2,1,0:T(8,128)(2,1)} copy(bf16[16,2,384,128]{3,1,2,0:T(2,128)(2,1)} %all-to-all-done) | data formatting | bytes 6291456 | tf_op jit(solution)/shard_map/all_to_all | solution.py:401
  211.6 24.2 %backward.1 = (f32[384,384]{1,0:T(8,128)S(1)}, f32[384,80]{1,0:T(8,128)S(1)}, f32[384,224]{1,0:T(8,128)S(1)}, f32[384,9]{1,0:T(8,128)S(1)}, f32[3,8,128]{2,1,0:T(8,128)S(1)}) custom-call(f32[8]{0:T(128)S(1)} %pad_maximum_fusion.coef, bf16[32,384,128]{2,1,0:T(8,128)(2,1)} %bitcast.38, bf16[384,384]{1,0:T(8,128)(2,1)S(1)} %copy-done, ...), custom_call_target="tpu_custom_call" | custom-call | flops 3000000000 | bytes 16000000 | tf_op jit(solution)/shard_map/backward/pallas_call | solution.py:372
  236.2 0.4 reshape.121
  236.8 0.2 reshape.122
  237.0 0.6 fusion.4
  240.3 1.6 concatenate.14
  241.9 1.2 reshape.123
  243.1 13.7 %all-to-all-start.3 = ((bf16[256,9,128]{2,1,0:T(8,128)(2,1)}), bf16[256,9,128]{2,1,0:T(8,128)(2,1)S(1)}, u32[]{:S(2)}, u32[]{:S(2)}) async-start(bf16[256,9,128]{2,1,0:T(8,128)(2,1)} %reshape.123), calls=%async_computation.3 | async-start | bytes 2097152 | tf_op jit(solution)/shard_map/all_to_all | solution.py:416
  256.8 1.2 reshape.128
  258.0 30.5 %all-to-all-done.3 = bf16[256,9,128]{2,1,0:T(8,128)(2,1)S(1)} async-done(((bf16[256,9,128]{2,1,0:T(8,128)(2,1)}), bf16[256,9,128]{2,1,0:T(8,128)(2,1)S(1)}, u32[]{:S(2)}, u32[]{:S(2)}) %all-to-all-start.3) | async-done | bytes 589856 | tf_op jit(solution)/shard_map/all_to_all | solution.py:416
  288.5 0.3 reduce_sum.53
  288.8 1.1 broadcast_in_dim.4
  289.9 5.8 %all-to-all-start.4 = ((bf16[256,9,128]{2,1,0:T(8,128)(2,1)}), bf16[256,9,128]{2,1,0:T(8,128)(2,1)S(1)}, u32[]{:S(2)}, u32[]{:S(2)}) async-start(bf16[256,9,128]{2,1,0:T(8,128)(2,1)} %broadcast_in_dim.4), calls=%async_computation.4 | async-start | bytes 2097152 | tf_op jit(solution)/shard_map/all_to_all | solution.py:420
  295.7 1.0 reshape.134
  296.7 0.2 reshape.146
  297.0 0.6 reshape.138
  297.6 29.7 %all-to-all-done.4 = bf16[256,9,128]{2,1,0:T(8,128)(2,1)S(1)} async-done(((bf16[256,9,128]{2,1,0:T(8,128)(2,1)}), bf16[256,9,128]{2,1,0:T(8,128)(2,1)S(1)}, u32[]{:S(2)}, u32[]{:S(2)}) %all-to-all-start.4) | async-done | bytes 589856 | tf_op jit(solution)/shard_map/all_to_all | solution.py:420
  327.3 0.3 reshape.124
  327.6 42.0 %slice.91 = bf16[73728,4]{1,0:T(8,128)(2,1)} reshape(bf16[256,9,128]{2,1,0:T(8,128)(2,1)S(1)} %all-to-all-done.4) | data formatting | bytes 1179648 | tf_op jit(solution)/shard_map/slice | solution.py:423
  369.6 1.2 convert_reduce_fusion
  371.0 0.9 copy.50
  372.0 1.0 reshape.133
  373.1 0.8 copy.49
  373.8 0.2 reshape.144
  374.1 0.6 reshape.136
  (55 shorter events, 2.4 us)
Async XLA Ops:
  0.6 47.7 %copy-start.9 = (bf16[128,256]{1,0:T(8,128)(2,1)S(1)}, bf16[128,256]{1,0:T(8,128)(2,1)}, u32[]{:S(2)}) copy-start(bf16[128,256]{1,0:T(8,128)(2,1)} %constant.19.clone.up) | copy-start | bytes 196612
  0.6 47.7 %copy-start.8 = (bf16[512,128]{1,0:T(8,128)(2,1)S(1)}, bf16[512,128]{1,0:T(8,128)(2,1)}, u32[]{:S(2)}) copy-start(bf16[512,128]{1,0:T(8,128)(2,1)} %constant.20.clone.pool) | copy-start | bytes 393220
  0.7 40.8 %copy-start.11 = (f32[4]{0:T(128)S(1)}, f32[4]{0:T(128)}, u32[]{:S(2)}) copy-start(f32[4]{0:T(128)} %param.25) | copy-start | bytes 52
  0.7 40.3 %copy-start = (bf16[384,384]{1,0:T(8,128)(2,1)S(1)}, bf16[384,384]{1,0:T(8,128)(2,1)}, u32[]{:S(2)}) copy-start(bf16[384,384]{1,0:T(8,128)(2,1)} %point.1) | copy-start | bytes 884740
  0.7 40.6 %copy-start.10 = (f32[3,3,384]{2,1,0:T(4,128)S(1)}, f32[3,3,384]{2,1,0:T(4,128)}, u32[]{:S(2)}) copy-start(f32[3,3,384]{2,1,0:T(4,128)} %param.24) | copy-start | bytes 41476
  30.5 17.8 %all-to-all-start.2 = ((bf16[16,64,224]{2,1,0:T(8,128)(2,1)}), bf16[16,64,224]{2,1,0:T(8,128)(2,1)S(1)}, u32[]{:S(2)}, u32[]{:S(2)}) async-start(bf16[16,64,224]{2,1,0:T(8,128)(2,1)} %bitcast.46), calls=%async_computation.2 | async-start | bytes 1048576 | tf_op jit(solution)/shard_map/all_to_all | solution.py:401
  41.8 41.8 %copy-start.1 = (bf16[16,2,80,128]{3,2,1,0:T(8,128)(2,1)}, bf16[16,2,80,128]{3,2,1,0:T(8,128)(2,1)S(1)}, u32[]{:S(2)}) copy-start(bf16[16,2,80,128]{3,2,1,0:T(8,128)(2,1)S(1)} %copy.41) | copy-start | bytes 1966084
  61.3 0.9 copy-start.2
  62.2 0.9 copy-start.3
  63.1 1.0 copy-start.4
  83.6 0.7 copy-start.5
  118.9 77.2 %all-to-all-start = ((bf16[16,2,384,128]{3,1,2,0:T(2,128)(2,1)}), bf16[16,2,384,128]{3,1,2,0:T(2,128)(2,1)}, u32[]{:S(2)}, u32[]{:S(2)}) async-start(bf16[16,2,384,128]{3,1,2,0:T(2,128)(2,1)} %bitcast.39), calls=%async_computation | async-start | bytes 6291456 | tf_op jit(solution)/shard_map/all_to_all | solution.py:401
  196.1 47.1 %all-to-all-start.6 = ((bf16[256,5,128]{2,1,0:T(8,128)(2,1)}), bf16[256,5,128]{2,1,0:T(8,128)(2,1)}, u32[]{:S(2)}, u32[]{:S(2)}) async-start(bf16[256,5,128]{2,1,0:T(8,128)(2,1)} %broadcast_in_dim.5), calls=%async_computation.6 | async-start | bytes 1048576 | tf_op jit(solution)/shard_map/all_to_all | solution.py:420
  207.2 4.4 %copy-start.6 = (bf16[2,128,256]{2,1,0:T(8,128)(2,1)S(1)}, bf16[2,128,256]{2,1,0:T(8,128)(2,1)}, u32[]{:S(2)}) copy-start(bf16[2,128,256]{2,1,0:T(8,128)(2,1)} %constant.21.clone.up) | copy-start | bytes 393220
  207.2 4.4 %copy-start.7 = (bf16[512,128]{1,0:T(8,128)(2,1)S(1)}, bf16[512,128]{1,0:T(8,128)(2,1)}, u32[]{:S(2)}) copy-start(bf16[512,128]{1,0:T(8,128)(2,1)} %constant.22.clone.pool) | copy-start | bytes 393220
  243.1 45.4 %all-to-all-start.3 = ((bf16[256,9,128]{2,1,0:T(8,128)(2,1)}), bf16[256,9,128]{2,1,0:T(8,128)(2,1)S(1)}, u32[]{:S(2)}, u32[]{:S(2)}) async-start(bf16[256,9,128]{2,1,0:T(8,128)(2,1)} %reshape.123), calls=%async_computation.3 | async-start | bytes 2097152 | tf_op jit(solution)/shard_map/all_to_all | solution.py:416
  289.9 37.4 %all-to-all-start.4 = ((bf16[256,9,128]{2,1,0:T(8,128)(2,1)}), bf16[256,9,128]{2,1,0:T(8,128)(2,1)S(1)}, u32[]{:S(2)}, u32[]{:S(2)}) async-start(bf16[256,9,128]{2,1,0:T(8,128)(2,1)} %broadcast_in_dim.4), calls=%async_computation.4 | async-start | bytes 2097152 | tf_op jit(solution)/shard_map/all_to_all | solution.py:420

commit v2 on v1

--- a/solution.py
+++ b/solution.py
@@ -2,9 +2,10 @@
 import jax.numpy as jnp
 import numpy as np
 from jax import lax
+from jax.experimental.layout import Layout, with_layout_constraint
 from jax.experimental import pallas as pl
 from jax.experimental.pallas import tpu as pltpu
-from jax.sharding import PartitionSpec as P
+from jax.sharding import Mesh, PartitionSpec as P
 
 EPSILON = 0.0001
 F = 384
@@ -14,7 +15,9 @@
 PAIRS = 8
 HALF = jnp.bfloat16
 WIDE = jnp.float32
-ALL = ("dp", "space")
+CHIPS = ("group", "space")
+HALF_ROWS = 1792
+ROW_MAJOR = Layout(major_to_minor=(0, 1, 2, 3))
 LIMIT = 50 * 1024 * 1024
 
 
@@ -86,19 +89,26 @@
     return 1.0 / (1.0 + jnp.exp(-values))
 
 
+def fine_pair(maps, s):
+    return maps[s, :80]
+
+
+def coarse_pair(maps, k):
+    return jnp.concatenate([maps[2 * k, 80:144], maps[2 * k + 1, 80:144]], axis=0)
+
+
 def forward_kernel(
-    coef, fine, coarse, lat_fine, lat_coarse, kern, up, pool,
+    coef, maps, lat_fine, lat_coarse, kern, up, pool,
     act_out, slope_out, depth_out, proj_out, pooled_out, proj, lifted,
 ):
-    lifted_low = nt(lat_coarse[...], coarse[...]).astype(HALF)
     for k in range(PAIRS):
-        pair = lifted_low[:, 128 * k : 128 * k + 128]
+        pair = nt(lat_coarse[...], coarse_pair(maps, k)).astype(HALF)
         proj_out[k] = pair
         both = nn(pair, up[...])
         lifted[2 * k] = both[:, :128]
         lifted[2 * k + 1] = both[:, 128:]
     for s in range(ROWS // 2):
-        both = nn(lat_fine[...], jnp.concatenate([fine[2 * s], fine[2 * s + 1]], axis=1))
+        both = nn(lat_fine[...], fine_pair(maps, s))
         proj[2 * s] = both[:, :128]
         proj[2 * s + 1] = both[:, 128:]
     own, above = coef[0], coef[1]
@@ -135,15 +145,16 @@
 
 
 def coarse_kernel(
-    coef, pooled_depth, proj, point_fine, point_fine_t, point_coarse, cotan, coarse, kern,
-    grad_point, grad_kern, grad_point_fine, quarter_back, grad_lat, sums,
-    pooled, active_s, gate_s, back_s, depth_s, pooled_back, own_back,
+    coef, pooled_depth, proj, point_fine, point_fine_t, point_coarse, cotan, maps, kern,
+    packed, grad_point_fine, quarter_back, grad_lat, sums,
+    grad_kern, pooled, active_s, gate_s, back_s, depth_s, pooled_back, own_back,
 ):
-    own, down, scale_own, scale_down = coef[2], coef[3], coef[4], coef[5]
+    own, down = coef[2], coef[3]
     for k in range(PAIRS):
         pooled[k] = nn(point_fine_t[...], pooled_depth[k]).astype(HALF).astype(WIDE)
         back_s[k] = nt(point_coarse[...], cotan[k]).astype(HALF).astype(WIDE)
     sums[...] = jnp.zeros_like(sums)
+    grad_kern[...] = jnp.zeros_like(grad_kern)
 
     def rows_of(cells, lane):
         turned = [pltpu.roll(c, 64, 1) for c in cells]
@@ -200,8 +211,8 @@
             slope = total * gate_s[k, at, :]
             sum_own = sum_own + slope * proj[k, at, :].astype(WIDE)
             sum_down = sum_down + slope * pooled[k, at, :]
-            pooled_back[k, at, :] = (scale_down * slope).astype(HALF)
-            own_back[k, at, :] = (scale_own * slope).astype(HALF)
+            pooled_back[k, at, :] = (down * slope).astype(HALF)
+            own_back[k, at, :] = (own * slope).astype(HALF)
         for u in range(3):
             for v in range(3):
                 grad_kern[at, 3 * u + v : 3 * u + v + 1] = lane_sum(weight[u][v])
@@ -215,19 +226,24 @@
     for k in range(PAIRS):
         point = accumulate(point, nn(depth_s[k], cotan[k]))
         point_f = accumulate(point_f, nt(pooled_depth[k], pooled_back[k]))
-        lat = accumulate(lat, nn(own_back[k], coarse[k]))
+        lat = accumulate(lat, nn(own_back[k], coarse_pair(maps, k)))
         quarter_back[k] = (0.25 * nn(point_fine[...], pooled_back[k])).astype(HALF)
-    grad_point[...] = point
+    for j in range(F // 128):
+        packed[F * j : F * j + F] = point[:, 128 * j : 128 * j + 128].astype(HALF)
+        taps = grad_kern[128 * j : 128 * j + 128].T[:16]
+        packed[3 * F + 16 * j : 3 * F + 16 * j + 16] = taps.astype(HALF)
     grad_point_fine[...] = point_f
     grad_lat[...] = lat
 
 
 def backward_kernel(
-    coef, cotan, point, quarter_back, act, steep, depth, fine, coarse, lat_fine, lat_coarse,
-    kern, up, pool, part_point, part_lat,
-    grad_point, grad_lat_fine, grad_lat_coarse, grad_kern, sums,
-    back, slope_s,
+    core, coef, cotan, point, quarter_back, act, steep, depth, maps, lat_fine, lat_coarse,
+    kern, up, pool, part_point, part_lat, packed_coarse, sums_coarse,
+    keep, send,
+    sums, packed, grad_kern, back, slope_s,
 ):
+    j = pl.program_id(0)
+    grad_kern[...] = jnp.zeros_like(grad_kern)
     for s in range(ROWS // 2):
         both = nn(
             jnp.concatenate([point[...], quarter_back[s // 2]], axis=1),
@@ -276,9 +292,7 @@
         for a in range(2):
             s = 2 * k + a
             two = jnp.concatenate([slope_s[2 * s], slope_s[2 * s + 1]], axis=1)
-            lat_f = accumulate(
-                lat_f, nt(two, jnp.concatenate([fine[2 * s], fine[2 * s + 1]], axis=1))
-            )
+            lat_f = accumulate(lat_f, nt(two, fine_pair(maps, s)))
             point_g = accumulate(
                 point_g,
                 nt(
@@ -288,15 +302,66 @@
             )
             pooled.append(two)
         lat_c = accumulate(
-            lat_c, nn(nn(jnp.concatenate(pooled, axis=1), pool[...]).astype(HALF), coarse[k])
+            lat_c,
+            nn(nn(jnp.concatenate(pooled, axis=1), pool[...]).astype(HALF), coarse_pair(maps, k)),
         )
-    grad_point[...] = point_g + part_point[...]
-    grad_lat_fine[...] = coef[6] * lat_f
-    grad_lat_coarse[...] = coef[7] * lat_c + part_lat[...]
+    point_g = (point_g + part_point[...]).astype(HALF)
+    for o in range(F // 128):
+        packed[128 * o : 128 * o + 128] = point_g[:, 128 * o : 128 * o + 128]
+    wide_f = jnp.concatenate([coef[0] * lat_f, jnp.zeros((FB, 48), WIDE)], axis=1)
+    packed[384:464] = wide_f.T[:80].astype(HALF)
+    packed[464:688] = (coef[1] * lat_c + part_lat[...]).T[:224].astype(HALF)
+    packed[688:704] = grad_kern[...].T[:16].astype(HALF)
     first = jnp.sum(lat_f * lat_fine[...].astype(WIDE), axis=0, keepdims=True)
     second = jnp.sum(lat_c * lat_coarse[...].astype(WIDE), axis=0, keepdims=True)
-    row = lax.broadcasted_iota(jnp.int32, (8, 128), 0)
-    sums[0] = jnp.where(row == 0, jnp.sum(first), jnp.where(row == 1, jnp.sum(second), 0.0))
+    total_first = jnp.sum(first) + jnp.where(j == 0, 0.0, sums[0])
+    total_second = jnp.sum(second) + jnp.where(j == 0, 0.0, sums[1])
+    sums[0] = total_first
+    sums[1] = total_second
+
+    def put(half, start, values):
+        at = pl.ds(start, values.shape[0])
+
+        @pl.when(core[0] == half)
+        def _():
+            keep[at] = values
+
+        @pl.when(core[0] != half)
+        def _():
+            send[at] = values
+
+    put(
+        jnp.where(j == F // FB - 1, 1, 0),
+        pl.multiple_of(jnp.where(j == 1, 704, 0), 16),
+        packed[...],
+    )
+
+    @pl.when(j == 0)
+    def _():
+        put(0, 1408, packed_coarse[:F])
+        put(1, 704, packed_coarse[F:])
+
+    @pl.when(j == F // FB - 1)
+    def _():
+        terms = [total_first, total_second, jnp.sum(sums_coarse[0]), jnp.sum(sums_coarse[1])]
+        mean_fine = coef[0] * terms[0] + coef[1] * terms[1]
+        mean_coarse = coef[2] * terms[2] + coef[3] * terms[3]
+        terms = [
+            (terms[0] - mean_fine) * coef[4],
+            (terms[1] - mean_fine) * coef[4],
+            (terms[2] - mean_coarse) * coef[5],
+            (terms[3] - mean_coarse) * coef[5],
+        ]
+        lane = lanes((16, 128))
+        row = jnp.zeros((16, 128), WIDE)
+        for i, term in enumerate(terms):
+            row = jnp.where(lane == i, term, row)
+        high = row.astype(HALF).astype(WIDE)
+        middle = (row - high).astype(HALF).astype(WIDE)
+        low = row - high - middle
+        row = high + pltpu.roll(middle, 4, 1) + pltpu.roll(low, 8, 1)
+        put(1, 1520, row.astype(HALF))
+        put(1, 1536, jnp.zeros((256, 128), HALF))
 
 
 def shaped(*shape, dtype=WIDE):
@@ -322,14 +387,14 @@
     return pl.BlockSpec((FB, width), lambda j: (j, 0))
 
 
-def forward(coef, fine, coarse, lat_fine, lat_coarse, kern):
+def forward(coef, maps, lat_fine, lat_coarse, kern):
     return pl.pallas_call(
         forward_kernel,
         name="forward",
         grid=(F // FB,),
         in_specs=[
-            SMEM, whole(ROWS, 80, 128), whole(1024, 224), cols_at(80), cols_at(224), cols_at(9),
-            whole(128, 256), whole(512, 128),
+            SMEM, whole(16, 144, 256), cols_at(80), cols_at(256), cols_at(9), whole(128, 256),
+            whole(512, 128),
         ],
         out_specs=[rows_at(ROWS), rows_at(ROWS), rows_at(ROWS), rows_at(PAIRS), rows_at(PAIRS)],
         out_shape=[shaped(ROWS, F, 128, dtype=HALF)] * 3 + [shaped(PAIRS, F, 128, dtype=HALF)] * 2,
@@ -340,89 +405,126 @@
         compiler_params=params(("arbitrary",)),
         cost_estimate=pl.CostEstimate(flops=10**9, bytes_accessed=12 * 10**6, transcendentals=10**6),
     )(
-        coef, fine, coarse, lat_fine, lat_coarse, kern,
+        coef, maps, lat_fine, lat_coarse, kern,
         jnp.asarray(upsampler(), HALF), jnp.asarray(pooler(0.25), HALF),
     )
 
 
-def coarse_node(coef, pooled_depth, proj, point_fine, point_coarse, cotan, coarse, kern):
+def coarse_node(coef, pooled_depth, proj, point_fine, point_coarse, cotan, maps, kern):
     return pl.pallas_call(
         coarse_kernel,
         name="coarse_node",
         in_specs=[SMEM] + [pl.BlockSpec(memory_space=pltpu.VMEM)] * 8,
-        out_specs=[pl.BlockSpec(memory_space=pltpu.VMEM)] * 6,
+        out_specs=[pl.BlockSpec(memory_space=pltpu.VMEM)] * 5,
         out_shape=[
-            shaped(F, F), shaped(F, 9), shaped(F, F), shaped(PAIRS, F, 128, dtype=HALF),
-            shaped(F, 224), shaped(2, CH, 128),
+            shaped(3 * F + 48, 128, dtype=HALF), shaped(F, F),
+            shaped(PAIRS, F, 128, dtype=HALF), shaped(F, 256), shaped(2, CH, 128),
         ],
-        scratch_shapes=[pltpu.VMEM((PAIRS, F, 128), WIDE)] * 4
+        scratch_shapes=[pltpu.VMEM((F, 128), WIDE)]
+        + [pltpu.VMEM((PAIRS, F, 128), WIDE)] * 4
         + [pltpu.VMEM((PAIRS, F, 128), HALF)] * 3,
         compiler_params=params(),
         cost_estimate=pl.CostEstimate(flops=10**9, bytes_accessed=5 * 10**6, transcendentals=10**6),
     )(
         coef, pooled_depth, proj, point_fine, point_fine.T, point_coarse,
-        cotan.reshape(PAIRS, 128, F), coarse.reshape(PAIRS, 128, 224), kern,
+        cotan.reshape(PAIRS, 128, F), maps, kern,
     )
 
 
 def backward(
-    coef, cotan, point, quarter_back, act, steep, depth, fine, coarse, lat_fine, lat_coarse,
-    kern, part_point, part_lat,
+    core, coef, cotan, point, quarter_back, act, steep, depth, maps, lat_fine, lat_coarse, kern,
+    part_point, part_lat, packed_coarse, sums_coarse,
 ):
     return pl.pallas_call(
         backward_kernel,
         name="backward",
         grid=(F // FB,),
         in_specs=[
-            SMEM, whole(ROWS, F, 128), cols_at(F), rows_at(PAIRS), rows_at(ROWS), rows_at(ROWS),
-            rows_at(ROWS), whole(ROWS, 80, 128), whole(PAIRS, 128, 224), cols_at(80),
-            cols_at(224), cols_at(9), whole(2, 128, 256), whole(512, 128), cols_at(F),
-            cols_at(224),
+            SMEM, SMEM, whole(ROWS, F, 128), cols_at(F), rows_at(PAIRS), rows_at(ROWS),
+            rows_at(ROWS), rows_at(ROWS), whole(16, 144, 256), cols_at(80), cols_at(256),
+            cols_at(9), whole(2, 128, 256), whole(512, 128), cols_at(F), cols_at(256),
+            whole(3 * F + 48, 128), whole(2, CH, 128),
         ],
-        out_specs=[
-            cols_at(F), cols_at(80), cols_at(224), cols_at(9),
-            pl.BlockSpec((1, 8, 128), lambda j: (j, 0, 0)),
-        ],
-        out_shape=[shaped(F, F), shaped(F, 80), shaped(F, 224), shaped(F, 9), shaped(F // FB, 8, 128)],
+        out_specs=[whole(HALF_ROWS, 128)] * 2,
+        out_shape=[shaped(HALF_ROWS, 128, dtype=HALF)] * 2,
         scratch_shapes=[
+            pltpu.SMEM((2,), WIDE),
+            pltpu.VMEM((704, 128), HALF),
+            pltpu.VMEM((FB, 128), WIDE),
             pltpu.VMEM((ROWS, FB, 128), WIDE),
             pltpu.VMEM((ROWS, FB, 128), HALF),
         ],
         compiler_params=params(("arbitrary",)),
         cost_estimate=pl.CostEstimate(flops=3 * 10**9, bytes_accessed=16 * 10**6, transcendentals=0),
     )(
-        coef, cotan, point, quarter_back, act, steep, depth, fine,
-        coarse.reshape(PAIRS, 128, 224), lat_fine, lat_coarse, kern,
-        jnp.asarray(upsampler_rows(), HALF), jnp.asarray(pooler(1.0), HALF), part_point, part_lat,
-    )
+        core, coef, cotan, point, quarter_back, act, steep, depth, maps, lat_fine, lat_coarse,
+        kern, jnp.asarray(upsampler_rows(), HALF), jnp.asarray(pooler(1.0), HALF), part_point,
+        part_lat, packed_coarse, sums_coarse,
+    )
+
+
+def unpack_kernel(
+    core, mine, other, lat_fine, lat_coarse, point_fine, point_coarse, kern_fine, kern_coarse, join,
+):
+    def spread(halves):
+        for j in range(F // FB):
+            at = slice(128 * j, 128 * j + 128)
+            rows, base = (halves[1], 0) if j == 2 else (halves[0], 704 * j)
+            for o in range(3):
+                low = base + 128 * o
+                point_fine[at, 128 * o : 128 * o + 128] = rows[low : low + 128].astype(WIDE)
+            lat_fine[:, at] = rows[base + 384 : base + 464].astype(WIDE)
+            lat_coarse[:, at] = rows[base + 464 : base + 688].astype(WIDE)
+            fine_taps = rows[base + 688 : base + 704].astype(WIDE)
+            low = 1472 + 16 * j
+            coarse_taps = halves[1][low : low + 16].astype(WIDE)
+            for u in range(3):
+                kern_fine[u, :, at] = fine_taps[3 * u : 3 * u + 3]
+                kern_coarse[u, :, at] = coarse_taps[3 * u : 3 * u + 3]
+            rows, low = (halves[1], 704 + F * (j - 1)) if j else (halves[0], 1408)
+            point_coarse[:, at] = rows[low : low + F].astype(WIDE)
+        last = halves[1][1520:1536].astype(WIDE)
+        join[...] = (last + pltpu.roll(last, 124, 1) + pltpu.roll(last, 120, 1))[:8]
+
+    @pl.when(core[0] == 0)
+    def _():
+        spread((mine, other))
+
+    @pl.when(core[0] != 0)
+    def _():
+        spread((other, mine))
+
+
+def unpack(core, mine, other):
+    return pl.pallas_call(
+        unpack_kernel,
+        name="unpack",
+        in_specs=[SMEM] + [pl.BlockSpec(memory_space=pltpu.VMEM)] * 2,
+        out_shape=[
+            shaped(80, F), shaped(224, F), shaped(F, F), shaped(F, F), shaped(3, 3, F),
+            shaped(3, 3, F), shaped(8, 128),
+        ],
+        compiler_params=params(),
+    )(core, mine, other)
 
 
 def to_images(values):
     return lax.all_to_all(values, "space", split_axis=0, concat_axis=0, tiled=True)
 
 
-def thirds(values):
-    high = values.astype(HALF)
-    rest = values - high.astype(WIDE)
-    middle = rest.astype(HALF)
-    return jnp.concatenate([high, middle, (rest - middle.astype(WIDE)).astype(HALF)])
-
-
-def total_over_devices(parts):
-    flat = jnp.concatenate([p.astype(HALF).reshape(-1) for p in parts])
-    count = lax.axis_size("dp") * lax.axis_size("space")
-    share = -(-flat.size // (count * 128)) * 128
-    flat = jnp.pad(flat, (0, count * share - flat.size)).reshape(count, share // 128, 128)
-    mine = lax.all_to_all(flat, ALL, split_axis=0, concat_axis=0, tiled=True)
-    mine = jnp.sum(mine.astype(WIDE), axis=0).astype(HALF)
-    mine = jnp.broadcast_to(mine[None], (count,) + mine.shape)
-    mine = lax.optimization_barrier(mine)
-    full = lax.all_to_all(mine, ALL, split_axis=0, concat_axis=0, tiled=True).reshape(-1)
-    out, start = [], 0
-    for p in parts:
-        out.append(full[start : start + p.size].reshape(p.shape).astype(WIDE))
-        start += p.size
-    return out
+def to_other_core(values):
+    return lax.ppermute(values, "core", [(0, 1), (1, 0)])
+
+
+def sum_over_devices(keep, send):
+    count = lax.axis_size("group") * lax.axis_size("space")
+    share = HALF_ROWS // (2 * count)
+    both = (keep.astype(WIDE) + to_other_core(send).astype(WIDE)).astype(HALF)
+    mine = lax.all_to_all(both.reshape(count, share, 2, 128), CHIPS, 0, 0, tiled=True)
+    mine = lax.optimization_barrier(jnp.sum(mine.astype(WIDE), axis=0)).astype(HALF)
+    mine = lax.optimization_barrier(jnp.broadcast_to(mine[None], (count,) + mine.shape))
+    mine = lax.all_to_all(mine, CHIPS, 0, 0, tiled=True).reshape(HALF_ROWS, 128)
+    return mine, to_other_core(mine)
 
 
 def body(
@@ -441,59 +543,45 @@
     fine_total = joining[0] + joining[1] + EPSILON
     coarse_total = joining[2] + joining[3] + EPSILON
     ratio = joining / jnp.stack([fine_total, fine_total, coarse_total, coarse_total])
-    coef = jnp.concatenate([ratio, ratio[2:], ratio[:2]])
-    coarse = to_images(jnp.transpose(coarse_map, (0, 2, 3, 1)).reshape(16, 64, 224))
-    fine = to_images(jnp.transpose(fine_map, (0, 2, 1, 3))).reshape(ROWS, 80, 128)
-    cotan = to_images(jnp.transpose(fine_cotan, (0, 2, 1, 3))).reshape(ROWS, F, 128)
+    coef = jnp.concatenate([ratio, jnp.stack([1.0 / fine_total, 1.0 / coarse_total])])
+    core = lax.axis_index("core").astype(jnp.int32)[None]
+    fine = fine_map.reshape(16, 80, 256)
+    coarse = jnp.transpose(coarse_map, (0, 2, 3, 1)).reshape(16, 64, 224)
+    maps = to_images(jnp.concatenate([fine, jnp.pad(coarse, ((0, 0), (0, 0), (0, 32)))], axis=1))
+    cotan = with_layout_constraint(jnp.transpose(fine_cotan, (0, 2, 1, 3)), ROW_MAJOR)
+    maps, cotan = lax.optimization_barrier((maps, cotan))
+    cotan = to_images(cotan).reshape(ROWS, F, 128)
     coarse_cot = jnp.transpose(coarse_cotan, (0, 2, 3, 1)).reshape(1024, F)
-    coarse = coarse.reshape(1024, 224)
-    lat_fine, lat_coarse = lateral_fine.T, lateral_coarse.T
+    lat_fine = lateral_fine.T
+    lat_coarse = jnp.pad(lateral_coarse.T, ((0, 0), (0, 32)))
     kern_fine = kernel_fine.reshape(9, F).T
     kern_coarse = kernel_coarse.reshape(9, F).T
     act, steep, depth, proj_coarse, pooled_depth = forward(
-        coef, fine, coarse, lat_fine, lat_coarse, kern_fine
-    )
-    grad_point_coarse, grad_kern_coarse, part_point, quarter_back, part_lat, sums_coarse = (
-        coarse_node(
-            coef, pooled_depth, proj_coarse, point_fine, point_coarse, coarse_cot, coarse,
-            kern_coarse,
-        )
-    )
-    grad_point_fine, grad_lat_fine, grad_lat_coarse, grad_kern_fine, sums_fine = backward(
-        coef, cotan, point_fine, quarter_back, act, steep, depth, fine, coarse, lat_fine,
-        lat_coarse, kern_fine, part_point, part_lat,
-    )
-    sums = jnp.concatenate([sums_fine[:, :2, 0].sum(axis=0), sums_coarse.sum(axis=(1, 2))])
-    mean_fine = ratio[0] * sums[0] + ratio[1] * sums[1]
-    mean_coarse = ratio[2] * sums[2] + ratio[3] * sums[3]
-    join_term = jnp.concatenate(
-        [(sums[:2] - mean_fine) / fine_total, (sums[2:] - mean_coarse) / coarse_total]
-    )
-    early = total_over_devices([grad_point_coarse, grad_kern_coarse])
-    late = total_over_devices(
-        [grad_point_fine, grad_lat_fine, grad_lat_coarse, grad_kern_fine, thirds(join_term)]
-    )
-    grad_joining = late[4].reshape(3, 4).sum(axis=0)
-    return (
-        late[1].T,
-        late[2].T,
-        late[0],
-        early[0],
-        late[3].T.reshape(3, 3, F),
-        early[1].T.reshape(3, 3, F),
-        grad_joining,
-    )
+        coef, maps, lat_fine, lat_coarse, kern_fine
+    )
+    packed_coarse, part_point, quarter_back, part_lat, sums_coarse = coarse_node(
+        coef, pooled_depth, proj_coarse, point_fine, point_coarse, coarse_cot, maps, kern_coarse
+    )
+    keep, send = backward(
+        core, coef, cotan, point_fine, quarter_back, act, steep, depth, maps, lat_fine,
+        lat_coarse, kern_fine, part_point, part_lat, packed_coarse, sums_coarse,
+    )
+    out = unpack(core, *sum_over_devices(keep, send))
+    return (*out[:6], out[6][0, :4])
 
 
 def solution(mesh):
+    dp, space = mesh.devices.shape
+    finer = Mesh(mesh.devices.reshape(dp // 2, 2, space), ("group", "core", "space"))
+    dp = ("group", "core")
     return jax.shard_map(
         body,
-        mesh=mesh,
+        mesh=finer,
         in_specs=(
-            P("dp", None, "space", None),
-            P("dp", None, "space", None),
-            P("dp", None, "space", None),
-            P(("dp", "space"), None, None, None),
+            P(dp, None, "space", None),
+            P(dp, None, "space", None),
+            P(dp, None, "space", None),
+            P((*dp, "space"), None, None, None),
             P(),
             P(),
             P(),

time: 376 us -> 210 us (0.56)
  waiting for transfers between devices: 135 us -> 60.6 us
  local copies, waits for them, and re-layouts: 69.3 us -> 10.5 us
  starting transfers between devices: 38.7 us -> 23.4 us
  blocking collectives: 63 us -> 50.1 us
  between operations: 8.76 us -> 3.53 us
    all_to_all x3 -> x0, waiting for transfers between devices: 60.2 us -> none  [the longest x1 30.5 us: total_over_devices(): mine = lax.all_to_all(flat, ALL, split_axis=0, concat_axis=0, tiled=True)]
    slice x4 -> x0, local copies, waits for them, and re-layouts: 43.3 us -> none  [the longest x1 42 us: total_over_devices(): out.append(full[start:start + p.size].reshape(p.shape).astype(WIDE))]
    all_to_all x3 -> x0, starting transfers between devices: 30.6 us -> none  [the longest x2 16.9 us: total_over_devices(): lax.all_to_all(mine, ALL, split_axis=0, concat_axis=0, tiled=True)]
    all_to_all x2, waiting for transfers between devices: 74.8 us -> 57.7 us  [to_images(): lax.all_to_all(values, 'space', split_axis=0, concat_axis=0, tiled=True)]
    all_to_all x2, blocking collectives: 63 us -> 50.1 us  [the longest x1 26.6 us: sum_over_devices(): lax.all_to_all(both.reshape(count, share, 2, 128), CHIPS, 0, 0, tiled=True)]
    all_to_all x2, starting transfers between devices: 8.07 us -> 17.2 us  [to_images(): lax.all_to_all(values, 'space', split_axis=0, concat_axis=0, tiled=True)]
    ppermute x0 -> x2, starting transfers between devices: none -> 6.2 us  [to_other_core(): return lax.ppermute(values, 'core', [(0, 1), (1, 0)])]
    all_to_all x2 -> x0, local copies, waits for them, and re-layouts: 4.44 us -> none  [to_images(): lax.all_to_all(values, 'space', split_axis=0, concat_axis=0, tiled=True)]
  transfers between devices with their start and end apart: 5 -> 4, of which waited for: 4 -> 4; matrix products, arithmetic and copies ran while one was open for 5% -> 3% of each run, Pallas kernels for 6% -> 15%
where the time goes in v2:
time: 210 us; the launch traced here: 209 us
  waiting for transfers between devices  60.6 us (29%)
  Pallas kernels  58.4 us (28%)
  blocking collectives  50.1 us (24%)
  starting transfers between devices  23.4 us (11%)
  local copies, waits for them, and re-layouts  10.5 us (5%)
  between operations  3.53 us (2%)
  other arithmetic  2.89 us (1%)
    all_to_all x2, waiting for transfers between devices, to_images(): lax.all_to_all(values, 'space', split_axis=0, concat_axis=0, tiled=True)  57.7 us
    all_to_all x1, blocking collectives, sum_over_devices(): lax.all_to_all(both.reshape(count, share, 2, 128), CHIPS, 0, 0, tiled=True)  26.6 us
    pallas_call x1, Pallas kernels, backward(): pl.pallas_call(backward_kernel, name='backward', grid=(F // FB,), in_spec...  25 us
    all_to_all x1, blocking collectives, sum_over_devices(): mine = lax.all_to_all(mine, CHIPS, 0, 0, tiled=True).reshape(HALF_ROWS, 128)  23.4 us
    pallas_call x1, Pallas kernels, coarse_node(): pl.pallas_call(coarse_kernel, name='coarse_node', in_specs=[SMEM] + [pl.B...  18.8 us
    all_to_all x2, starting transfers between devices, to_images(): lax.all_to_all(values, 'space', split_axis=0, concat_axis=0, tiled=True)  17.2 us
    pallas_call x1, Pallas kernels, forward(): pl.pallas_call(forward_kernel, name='forward', grid=(F // FB,), in_specs=...  13.4 us
    unnamed x30, local copies, waits for them, and re-layouts  6.64 us
  transfers between devices with their start and end apart: 4, of which 4 were waited for; matrix products, arithmetic and copies ran while one was open for 3% of the time, Pallas kernels for 15%

profile of v2, /device:TPU:1, one launch (start us, length us, event | category | flops | bytes accessed | tf_op | source)
XLA Modules:
  0.0 209.4 jit_solution(5449415994868905024)
XLA Ops:
  0.6 2.2 %reshape.50 = bf16[16,80,256]{2,1,0:T(8,128)(2,1)S(1)} reshape(bf16[16,80,2,128]{3,2,1,0:T(2,128)(2,1)} %param.15) | data formatting | bytes 1310720 | tf_op jit(solution)/shard_map/reshape | solution.py:548
  2.9 2.2 %fusion.1 = bf16[16,144,256]{2,1,0:T(8,128)(2,1)} fusion(bf16[16,64,224]{2,1,0:T(8,128)(2,1)} %bitcast.34, bf16[16,80,256]{2,1,0:T(8,128)(2,1)S(1)} %reshape.50), kind=kLoop, calls=%fused_computation.3 | loop fusion | flops 3538944 | bytes 2293760 | tf_op jit(solution)/shard_map/concatenate | solution.py:550
  5.0 10.1 %all-to-all-start = ((bf16[16,144,256]{2,1,0:T(8,128)(2,1)}), bf16[16,144,256]{2,1,0:T(8,128)(2,1)S(1)}, u32[]{:S(2)}, u32[]{:S(2)}) async-start(bf16[16,144,256]{2,1,0:T(8,128)(2,1)} %fusion.1), calls=%async_computation | async-start | bytes 2359296 | tf_op jit(solution)/shard_map/all_to_all | solution.py:512
  15.2 4.3 %copy.37 = bf16[16,384,2,128]{3,1,2,0:T(8,128)(2,1)} copy(bf16[16,384,2,128]{3,2,1,0:T(2,128)(2,1)} %param.17) | data formatting | bytes 6291456 | tf_op args[2]
  19.5 23.3 %all-to-all-done.maps = bf16[16,144,256]{2,1,0:T(8,128)(2,1)S(1)} async-done(((bf16[16,144,256]{2,1,0:T(8,128)(2,1)}), bf16[16,144,256]{2,1,0:T(8,128)(2,1)S(1)}, u32[]{:S(2)}, u32[]{:S(2)}) %all-to-all-start) | async-done | bytes 1179680 | tf_op jit(solution)/shard_map/all_to_all | solution.py:512
  42.8 0.0 copy-start.9
  42.8 0.0 copy-start.8
  42.8 0.0 copy-start.1
  42.8 0.0 copy-start.6
  42.8 0.0 copy-start.7
  42.8 7.1 %all-to-all-start.1 = ((bf16[16,2,384,128]{3,2,1,0:T(8,128)(2,1)}), bf16[16,2,384,128]{3,2,1,0:T(8,128)(2,1)}, u32[]{:S(2)}, u32[]{:S(2)}) async-start(bf16[16,2,384,128]{3,2,1,0:T(8,128)(2,1)} %bitcast.30), calls=%async_computation.1 | async-start | bytes 6291456 | tf_op jit(solution)/shard_map/all_to_all | solution.py:512
  49.9 0.0 copy-done.12
  49.9 0.6 fusion.2
  53.2 0.0 copy-done.10
  53.2 0.0 copy-done.11
  53.3 0.0 copy-done.9
  53.3 0.1 copy.31
  53.4 0.1 copy.35
  53.6 0.1 copy.33
  53.7 0.0 copy-done.8
  53.7 0.1 copy.32
  53.9 0.0 copy-done.1
  53.9 0.2 copy.34
  54.1 0.0 copy-start.3
  54.1 0.1 maximum_divide_fusion
  54.2 0.1 pad_maximum_fusion.coef
  54.3 0.0 copy-done
  54.3 0.0 copy-done.6
  54.3 0.0 copy-done.7
  54.3 13.4 %forward.1 = (bf16[32,384,128]{2,1,0:T(8,128)(2,1)}, bf16[32,384,128]{2,1,0:T(8,128)(2,1)}, bf16[32,384,128]{2,1,0:T(8,128)(2,1)}, bf16[8,384,128]{2,1,0:T(8,128)(2,1)S(1)}, bf16[8,384,128]{2,1,0:T(8,128)(2,1)S(1)}) custom-call(f32[6]{0:T(128)S(1)} %pad_maximum_fusion.coef, bf16[16,144,256]{2,1,0:T(8,128)(2,1)S(1)} %all-to-all-done.maps, ...), custom_call_target="tpu_custom_call" | custom-call | flops 1000000000 | bytes 12000000 | tf_op jit(solution)/shard_map/forward/pallas_call | solution.py:391
  67.7 0.9 copy-done.2
  68.6 0.0 copy-done.3
  68.6 18.8 %coarse_node.1 = (bf16[1200,128]{1,0:T(8,128)(2,1)S(1)}, f32[384,384]{1,0:T(8,128)S(1)}, bf16[8,384,128]{2,1,0:T(8,128)(2,1)S(1)}, f32[384,256]{1,0:T(8,128)S(1)}, f32[2,16,128]{2,1,0:T(8,128)S(1)}) custom-call(f32[6]{0:T(128)S(1)} %pad_maximum_fusion.coef, bf16[8,384,128]{2,1,0:T(8,128)(2,1)S(1)} %get-tuple-element.30.pooled_depth, ...), custom_call_target="tpu_custom_call" | custom-call | flops 1000000000 | bytes 5000000 | tf_op jit(solution)/shard_map/coarse_node/pallas_call | solution.py:414
  87.3 34.4 %all-to-all-done.1 = bf16[16,2,384,128]{3,2,1,0:T(8,128)(2,1)} async-done(((bf16[16,2,384,128]{3,2,1,0:T(8,128)(2,1)}), bf16[16,2,384,128]{3,2,1,0:T(8,128)(2,1)}, u32[]{:S(2)}, u32[]{:S(2)}) %all-to-all-start.1) | async-done | bytes 3145760 | tf_op jit(solution)/shard_map/all_to_all | solution.py:512
  121.7 0.0 copy-done.4
  121.8 0.9 copy-done.5
  122.7 25.0 %backward.1 = (bf16[1792,128]{1,0:T(8,128)(2,1)S(1)}, bf16[1792,128]{1,0:T(8,128)(2,1)S(1)}) custom-call(s32[1]{0:T(128)} %bitcast.core, f32[6]{0:T(128)S(1)} %pad_maximum_fusion.coef, bf16[32,384,128]{2,1,0:T(8,128)(2,1)} %bitcast.5.cotan, bf16[384,384]{1,0:T(8,128)(2,1)S(1)} %copy-done.1, bf16[8,384,128]{2,1,0:T(8,128)(2,1)S(1)} %get-tuple-element.32.quarter_back, ...), custom_call_target="tpu_custom_call" | custom-call | flops 3000000000 | bytes 16000000 | tf_op jit(solution)/shard_map/backward/pallas_call | solution.py:438
  147.7 2.4 %collective-permute-start = (bf16[1792,128]{1,0:T(8,128)(2,1)S(1)}, bf16[1792,128]{1,0:T(8,128)(2,1)S(1)}, u32[]{:S(2)}, u32[]{:S(2)}) collective-permute-start(bf16[1792,128]{1,0:T(8,128)(2,1)S(1)} %get-tuple-element.41), channel_id=1, source_target_pairs={{0,16},{16,0},{1,17},{17,1},{2,18},{18,2},{3,19},{19,3},{4,20},{20... | collective-permute-start | bytes 1376264 | tf_op jit(solution)/shard_map/ppermute | solution.py:516
  150.1 1.4 collective-permute-done
  151.5 0.1 add_convert_fusion
  151.7 26.6 %all_to_all.20 = bf16[128,7,2,128]{3,2,1,0:T(2,128)(2,1)S(1)} all-to-all(bf16[128,7,2,128]{3,2,1,0:T(2,128)(2,1)S(1)} %bitcast.31), channel_id=1, replica_groups=mesh['group'=8,'core'=2,'space'=16] {'group','space'}, dimensions={0} | all-to-all | bytes 917504 | tf_op jit(solution)/shard_map/all_to_all | solution.py:523
  178.3 0.4 convert_reduce_fusion
  178.7 0.2 broadcast_in_dim.10
  178.9 23.4 %all_to_all.21 = bf16[128,7,2,128]{3,2,1,0:T(2,128)(2,1)S(1)} all-to-all(bf16[128,7,2,128]{3,2,1,0:T(2,128)(2,1)S(1)} %broadcast_in_dim.10), channel_id=1, replica_groups=mesh['group'=8,'core'=2,'space'=16] {'group','space'}, dimensions={0} | all-to-all | bytes 917504 | tf_op jit(solution)/shard_map/all_to_all | solution.py:526
  202.4 3.8 %collective-permute-start.1 = (bf16[1792,128]{1,0:T(8,128)(2,1)S(1)}, bf16[1792,128]{1,0:T(8,128)(2,1)S(1)}, u32[]{:S(2)}, u32[]{:S(2)}) collective-permute-start(bf16[1792,128]{1,0:T(8,128)(2,1)S(1)} %bitcast.22), channel_id=1, source_target_pairs={{0,16},{16,0},{1,17},{17,1},{2,18},{18,2},{3,19},{19,3},{4,20},{20... | collective-permute-start | bytes 1376264 | tf_op jit(solution)/shard_map/ppermute | solution.py:516
  206.2 1.4 collective-permute-done.1.other
  207.6 1.3 unpack.1
  208.9 0.5 slice_bitcast_fusion
  (10 shorter events, 0.1 us)
Async XLA Ops:
  5.0 37.7 %all-to-all-start = ((bf16[16,144,256]{2,1,0:T(8,128)(2,1)}), bf16[16,144,256]{2,1,0:T(8,128)(2,1)S(1)}, u32[]{:S(2)}, u32[]{:S(2)}) async-start(bf16[16,144,256]{2,1,0:T(8,128)(2,1)} %fusion.1), calls=%async_computation | async-start | bytes 2359296 | tf_op jit(solution)/shard_map/all_to_all | solution.py:512
  42.8 11.5 %copy-start = (bf16[16,144,256]{2,1,0:T(8,128)(2,1)}, bf16[16,144,256]{2,1,0:T(8,128)(2,1)S(1)}, u32[]{:S(2)}) copy-start(bf16[16,144,256]{2,1,0:T(8,128)(2,1)S(1)} %all-to-all-done.maps) | copy-start | bytes 3538948
  42.8 7.2 %copy-start.12 = (f32[4]{0:T(128)S(1)}, f32[4]{0:T(128)}, u32[]{:S(2)}) copy-start(f32[4]{0:T(128)} %param.25) | copy-start | bytes 52
  42.8 10.4 %copy-start.10 = (f32[3,3,384]{2,1,0:T(4,128)S(1)}, f32[3,3,384]{2,1,0:T(4,128)}, u32[]{:S(2)}) copy-start(f32[3,3,384]{2,1,0:T(4,128)} %param.23) | copy-start | bytes 41476
  42.8 10.5 %copy-start.11 = (f32[3,3,384]{2,1,0:T(4,128)S(1)}, f32[3,3,384]{2,1,0:T(4,128)}, u32[]{:S(2)}) copy-start(f32[3,3,384]{2,1,0:T(4,128)} %param.24) | copy-start | bytes 41476
  42.8 10.5 %copy-start.9 = (bf16[80,384]{1,0:T(8,128)(2,1)S(1)}, bf16[80,384]{1,0:T(8,128)(2,1)}, u32[]{:S(2)}) copy-start(bf16[80,384]{1,0:T(8,128)(2,1)} %param.19) | copy-start | bytes 184324
  42.8 10.9 %copy-start.8 = (bf16[224,384]{1,0:T(8,128)(2,1)S(1)}, bf16[224,384]{1,0:T(8,128)(2,1)}, u32[]{:S(2)}) copy-start(bf16[224,384]{1,0:T(8,128)(2,1)} %param.20) | copy-start | bytes 516100
  42.8 11.1 %copy-start.1 = (bf16[384,384]{1,0:T(8,128)(2,1)S(1)}, bf16[384,384]{1,0:T(8,128)(2,1)}, u32[]{:S(2)}) copy-start(bf16[384,384]{1,0:T(8,128)(2,1)} %point.1) | copy-start | bytes 884740
  42.8 11.5 %copy-start.6 = (bf16[512,128]{1,0:T(8,128)(2,1)S(1)}, bf16[512,128]{1,0:T(8,128)(2,1)}, u32[]{:S(2)}) copy-start(bf16[512,128]{1,0:T(8,128)(2,1)} %constant.28.clone.pool) | copy-start | bytes 393220
  42.8 11.5 %copy-start.7 = (bf16[128,256]{1,0:T(8,128)(2,1)S(1)}, bf16[128,256]{1,0:T(8,128)(2,1)}, u32[]{:S(2)}) copy-start(bf16[128,256]{1,0:T(8,128)(2,1)} %constant.27.clone.up) | copy-start | bytes 196612
  42.8 78.9 %all-to-all-start.1 = ((bf16[16,2,384,128]{3,2,1,0:T(8,128)(2,1)}), bf16[16,2,384,128]{3,2,1,0:T(8,128)(2,1)}, u32[]{:S(2)}, u32[]{:S(2)}) async-start(bf16[16,2,384,128]{3,2,1,0:T(8,128)(2,1)} %bitcast.30), calls=%async_computation.1 | async-start | bytes 6291456 | tf_op jit(solution)/shard_map/all_to_all | solution.py:512
  54.1 14.5 %copy-start.3 = (bf16[384,384]{1,0:T(8,128)(2,1)S(1)}, bf16[384,384]{1,0:T(8,128)(2,1)}, u32[]{:S(2)}) copy-start(bf16[384,384]{1,0:T(8,128)(2,1)} %point_coarse.1) | copy-start | bytes 884740
  67.7 0.9 copy-start.2
  68.6 53.2 %copy-start.4 = (bf16[512,128]{1,0:T(8,128)(2,1)S(1)}, bf16[512,128]{1,0:T(8,128)(2,1)}, u32[]{:S(2)}) copy-start(bf16[512,128]{1,0:T(8,128)(2,1)} %constant.30.clone.pool) | copy-start | bytes 393220
  121.8 0.9 copy-start.5
  147.7 3.9 %collective-permute-start = (bf16[1792,128]{1,0:T(8,128)(2,1)S(1)}, bf16[1792,128]{1,0:T(8,128)(2,1)S(1)}, u32[]{:S(2)}, u32[]{:S(2)}) collective-permute-start(bf16[1792,128]{1,0:T(8,128)(2,1)S(1)} %get-tuple-element.41), channel_id=1, source_target_pairs={{0,16},{16,0},{1,17},{17,1},{2,18},{18,2},{3,19},{19,3},{4,20},{20... | collective-permute-start | bytes 1376264 | tf_op jit(solution)/shard_map/ppermute | solution.py:516
  202.4 5.2 %collective-permute-start.1 = (bf16[1792,128]{1,0:T(8,128)(2,1)S(1)}, bf16[1792,128]{1,0:T(8,128)(2,1)S(1)}, u32[]{:S(2)}, u32[]{:S(2)}) collective-permute-start(bf16[1792,128]{1,0:T(8,128)(2,1)S(1)} %bitcast.22), channel_id=1, source_target_pairs={{0,16},{16,0},{1,17},{17,1},{2,18},{18,2},{3,19},{19,3},{4,20},{20... | collective-permute-start | bytes 1376264 | tf_op jit(solution)/shard_map/ppermute | solution.py:516

commit v3 on v2

--- a/solution.py
+++ b/solution.py
@@ -15,7 +15,8 @@
 PAIRS = 8
 HALF = jnp.bfloat16
 WIDE = jnp.float32
-CHIPS = ("group", "space")
+SPACE = ("z", "y")
+LEVEL = ("group", "y")
 HALF_ROWS = 1792
 ROW_MAJOR = Layout(major_to_minor=(0, 1, 2, 3))
 LIMIT = 50 * 1024 * 1024
@@ -95,6 +96,14 @@
 
 def coarse_pair(maps, k):
     return jnp.concatenate([maps[2 * k, 80:144], maps[2 * k + 1, 80:144]], axis=0)
+
+
+def join_kernel(fine, coarse, maps):
+    for i in range(maps.shape[0]):
+        maps[i, :80] = fine[i].reshape(80, 256)
+        maps[i, 80:, :128] = coarse[i, :, :128]
+        maps[i, 80:, 128:224] = coarse[i, :, 128:]
+        maps[i, 80:, 224:] = jnp.zeros((64, 32), HALF)
 
 
 def forward_kernel(
@@ -237,131 +246,147 @@
 
 
 def backward_kernel(
-    core, coef, cotan, point, quarter_back, act, steep, depth, maps, lat_fine, lat_coarse,
-    kern, up, pool, part_point, part_lat, packed_coarse, sums_coarse,
+    core, coef, cotan_far, act_far, steep_far, depth_far, point, quarter_back, maps, lat_fine,
+    lat_coarse, kern, up, pool, part_point, part_lat, packed_coarse, sums_coarse,
     keep, send,
-    sums, packed, grad_kern, back, slope_s,
+    cotan, act, steep, depth, halves, grad_kern, grad_point, back, slope_s, arrived,
 ):
-    j = pl.program_id(0)
+    quarter = ROWS // 4
+    share = F // PAIRS
+
+    def of_cotan(q):
+        at = pl.ds(quarter * q, quarter)
+        return pltpu.make_async_copy(cotan_far.at[at], cotan.at[at], arrived.at[q])
+
+    def of_step(step):
+        at = pl.ds(pl.multiple_of(share * step, 16), share)
+        rows = pl.ds(4 * step, 4)
+        return [
+            pltpu.make_async_copy(act_far.at[:, at], act.at[:, at], arrived.at[4 + step]),
+            pltpu.make_async_copy(steep_far.at[:, at], steep.at[:, at], arrived.at[12 + step]),
+            pltpu.make_async_copy(depth_far.at[rows], depth.at[rows], arrived.at[20 + step]),
+        ]
+
+    for q in range(4):
+        of_cotan(q).start()
+    for step in range(PAIRS):
+        for copy in of_step(step):
+            copy.start()
     grad_kern[...] = jnp.zeros_like(grad_kern)
+    grad_point[...] = part_point[...]
+    halves[0, 1408:] = packed_coarse[:F]
+    halves[1, 704:1520] = packed_coarse[F:]
+    halves[1, 1536:] = jnp.zeros((256, 128), HALF)
+
     for s in range(ROWS // 2):
+        if 2 * s % quarter == 0:
+            of_cotan(2 * s // quarter).wait()
         both = nn(
             jnp.concatenate([point[...], quarter_back[s // 2]], axis=1),
             jnp.concatenate(
                 [jnp.concatenate([cotan[2 * s], cotan[2 * s + 1]], axis=1), up[s % 2]], axis=0
             ),
         )
-        back[2 * s] = both[:, :128]
-        back[2 * s + 1] = both[:, 128:]
-
-    @pl.loop(0, FB // CH)
+        back[2 * s] = both[:, :128].astype(HALF)
+        back[2 * s + 1] = both[:, 128:].astype(HALF)
+
+    @pl.loop(0, PAIRS)
     def _(step):
-        start = pl.multiple_of(step * CH, CH)
-        at = pl.ds(start, CH)
-        taps = taps_of(kern, start)
+        for copy in of_step(step):
+            copy.wait()
+        grad_point[...] += nt(
+            jnp.concatenate([depth[4 * step + a] for a in range(4)], axis=1),
+            jnp.concatenate([cotan[4 * step + a] for a in range(4)], axis=1),
+        )
         lane = lanes((CH, 128))
-        weight = [[None] * 3 for _ in range(3)]
-        sides = {}
-        for r in range(ROWS + 1):
-            if r < ROWS:
-                sides[r] = side_fine(back[r, at, :], lane)
-            if r >= 1:
-                active = act[r - 1, at, :].astype(WIDE)
-                total = None
-                for u in range(3):
-                    if r - u not in sides:
-                        continue
-                    for v in range(3):
-                        shifted = sides[r - u][2 - v]
-                        term = taps[u][v] * shifted
-                        total = term if total is None else total + term
-                        more = active * shifted
-                        weight[u][v] = more if weight[u][v] is None else weight[u][v] + more
-                slope_s[r - 1, at, :] = (total * steep[r - 1, at, :].astype(WIDE)).astype(HALF)
-                sides.pop(r - 2, None)
-        for u in range(3):
-            for v in range(3):
-                grad_kern[at, 3 * u + v : 3 * u + v + 1] = lane_sum(weight[u][v])
+        first_lane, last_lane = lane == 0, lane == 127
+        for part in range(F // (CH * PAIRS)):
+            start = pl.multiple_of(step * (F // PAIRS) + part * CH, CH)
+            at = pl.ds(start, CH)
+            taps = [
+                [jnp.where(last_lane, 0.0, left), middle, jnp.where(first_lane, 0.0, right)]
+                for left, middle, right in taps_of(kern, start)
+            ]
+            weight = [[None] * 3 for _ in range(3)]
+            sides = {}
+            for r in range(ROWS + 1):
+                if r < ROWS:
+                    cells = back[r, at, :]
+                    turned = (pltpu.roll(cells, 127, 1), cells, pltpu.roll(cells, 1, 1))
+                    sides[r] = [c.astype(WIDE) for c in turned]
+                if r >= 1:
+                    active = act[r - 1, at, :].astype(WIDE)
+                    total = None
+                    for u in range(3):
+                        if r - u not in sides:
+                            continue
+                        for v in range(3):
+                            shifted = sides[r - u][v]
+                            term = taps[u][v] * shifted
+                            total = term if total is None else total + term
+                            more = active * shifted
+                            weight[u][v] = more if weight[u][v] is None else weight[u][v] + more
+                    slope_s[r - 1, at, :] = (total * steep[r - 1, at, :].astype(WIDE)).astype(HALF)
+                    sides.pop(r - 2, None)
+            for u in range(3):
+                cleared = [
+                    jnp.where(last_lane, 0.0, weight[u][0]),
+                    weight[u][1],
+                    jnp.where(first_lane, 0.0, weight[u][2]),
+                ]
+                for v in range(3):
+                    grad_kern[at, 3 * u + v : 3 * u + v + 1] = lane_sum(cleared[v])
 
     def accumulate(total, term):
         return term if total is None else total + term
 
-    point_g, lat_f, lat_c = None, None, None
+    lat_f, lat_c = None, None
     for k in range(PAIRS):
-        pooled = []
-        for a in range(2):
-            s = 2 * k + a
-            two = jnp.concatenate([slope_s[2 * s], slope_s[2 * s + 1]], axis=1)
-            lat_f = accumulate(lat_f, nt(two, fine_pair(maps, s)))
-            point_g = accumulate(
-                point_g,
-                nt(
-                    jnp.concatenate([depth[2 * s], depth[2 * s + 1]], axis=1),
-                    jnp.concatenate([cotan[2 * s], cotan[2 * s + 1]], axis=1),
-                ),
-            )
-            pooled.append(two)
-        lat_c = accumulate(
-            lat_c,
-            nn(nn(jnp.concatenate(pooled, axis=1), pool[...]).astype(HALF), coarse_pair(maps, k)),
-        )
-    point_g = (point_g + part_point[...]).astype(HALF)
-    for o in range(F // 128):
-        packed[128 * o : 128 * o + 128] = point_g[:, 128 * o : 128 * o + 128]
-    wide_f = jnp.concatenate([coef[0] * lat_f, jnp.zeros((FB, 48), WIDE)], axis=1)
-    packed[384:464] = wide_f.T[:80].astype(HALF)
-    packed[464:688] = (coef[1] * lat_c + part_lat[...]).T[:224].astype(HALF)
-    packed[688:704] = grad_kern[...].T[:16].astype(HALF)
-    first = jnp.sum(lat_f * lat_fine[...].astype(WIDE), axis=0, keepdims=True)
-    second = jnp.sum(lat_c * lat_coarse[...].astype(WIDE), axis=0, keepdims=True)
-    total_first = jnp.sum(first) + jnp.where(j == 0, 0.0, sums[0])
-    total_second = jnp.sum(second) + jnp.where(j == 0, 0.0, sums[1])
-    sums[0] = total_first
-    sums[1] = total_second
-
-    def put(half, start, values):
-        at = pl.ds(start, values.shape[0])
-
-        @pl.when(core[0] == half)
-        def _():
-            keep[at] = values
-
-        @pl.when(core[0] != half)
-        def _():
-            send[at] = values
-
-    put(
-        jnp.where(j == F // FB - 1, 1, 0),
-        pl.multiple_of(jnp.where(j == 1, 704, 0), 16),
-        packed[...],
-    )
-
-    @pl.when(j == 0)
-    def _():
-        put(0, 1408, packed_coarse[:F])
-        put(1, 704, packed_coarse[F:])
-
-    @pl.when(j == F // FB - 1)
-    def _():
-        terms = [total_first, total_second, jnp.sum(sums_coarse[0]), jnp.sum(sums_coarse[1])]
-        mean_fine = coef[0] * terms[0] + coef[1] * terms[1]
-        mean_coarse = coef[2] * terms[2] + coef[3] * terms[3]
-        terms = [
-            (terms[0] - mean_fine) * coef[4],
-            (terms[1] - mean_fine) * coef[4],
-            (terms[2] - mean_coarse) * coef[5],
-            (terms[3] - mean_coarse) * coef[5],
-        ]
-        lane = lanes((16, 128))
-        row = jnp.zeros((16, 128), WIDE)
-        for i, term in enumerate(terms):
-            row = jnp.where(lane == i, term, row)
-        high = row.astype(HALF).astype(WIDE)
-        middle = (row - high).astype(HALF).astype(WIDE)
-        low = row - high - middle
-        row = high + pltpu.roll(middle, 4, 1) + pltpu.roll(low, 8, 1)
-        put(1, 1520, row.astype(HALF))
-        put(1, 1536, jnp.zeros((256, 128), HALF))
+        four = jnp.concatenate([slope_s[4 * k + a] for a in range(4)], axis=1)
+        both = jnp.concatenate([fine_pair(maps, 2 * k), fine_pair(maps, 2 * k + 1)], axis=1)
+        lat_f = accumulate(lat_f, nt(four, both))
+        lat_c = accumulate(lat_c, nn(nn(four, pool[...]).astype(HALF), coarse_pair(maps, k)))
+    point_t = grad_point[...].astype(HALF)
+    wide_f = jnp.concatenate([coef[0] * lat_f, jnp.zeros((F, 48), WIDE)], axis=1)
+    lat_f_t = wide_f.T[:80].astype(HALF)
+    lat_c_t = (coef[1] * lat_c + part_lat[...]).T[:224].astype(HALF)
+    kern_t = grad_kern[...].T[:16].astype(HALF)
+    for j in range(F // 128):
+        at = slice(128 * j, 128 * j + 128)
+        half, base = (1, 0) if j == 2 else (0, 704 * j)
+        for o in range(F // 128):
+            low = base + 128 * o
+            halves[half, low : low + 128] = point_t[at, 128 * o : 128 * o + 128]
+        halves[half, base + 384 : base + 464] = lat_f_t[:, at]
+        halves[half, base + 464 : base + 688] = lat_c_t[:, at]
+        halves[half, base + 688 : base + 704] = kern_t[:, at]
+
+    terms = [
+        jnp.sum(lat_f * lat_fine[...].astype(WIDE)),
+        jnp.sum(lat_c * lat_coarse[...].astype(WIDE)),
+        jnp.sum(sums_coarse[0]),
+        jnp.sum(sums_coarse[1]),
+    ]
+    mean_fine = coef[0] * terms[0] + coef[1] * terms[1]
+    mean_coarse = coef[2] * terms[2] + coef[3] * terms[3]
+    terms = [
+        (terms[0] - mean_fine) * coef[4],
+        (terms[1] - mean_fine) * coef[4],
+        (terms[2] - mean_coarse) * coef[5],
+        (terms[3] - mean_coarse) * coef[5],
+    ]
+    lane = lanes((16, 128))
+    row = jnp.zeros((16, 128), WIDE)
+    for i, term in enumerate(terms):
+        row = jnp.where(lane == i, term, row)
+    high = row.astype(HALF).astype(WIDE)
+    middle = (row - high).astype(HALF).astype(WIDE)
+    low = row - high - middle
+    row = high + pltpu.roll(middle, 4, 1) + pltpu.roll(low, 8, 1)
+    halves[1, 1520:1536] = row.astype(HALF)
+
+    keep[...] = halves[core[0]]
+    send[...] = halves[1 - core[0]]
 
 
 def shaped(*shape, dtype=WIDE):
@@ -385,6 +410,22 @@
 
 def cols_at(width):
     return pl.BlockSpec((FB, width), lambda j: (j, 0))
+
+
+def join_maps(fine, coarse):
+    step = 4
+    return pl.pallas_call(
+        join_kernel,
+        name="join_maps",
+        grid=(16 // step,),
+        in_specs=[
+            pl.BlockSpec((step, 80, 2, 128), lambda i: (i, 0, 0, 0)),
+            pl.BlockSpec((step, 64, 224), lambda i: (i, 0, 0)),
+        ],
+        out_specs=pl.BlockSpec((step, 144, 256), lambda i: (i, 0, 0)),
+        out_shape=shaped(16, 144, 256, dtype=HALF),
+        compiler_params=params(("arbitrary",)),
+    )(fine, coarse)
 
 
 def forward(coef, maps, lat_fine, lat_coarse, kern):
@@ -435,31 +476,29 @@
     core, coef, cotan, point, quarter_back, act, steep, depth, maps, lat_fine, lat_coarse, kern,
     part_point, part_lat, packed_coarse, sums_coarse,
 ):
+    far = pl.BlockSpec(memory_space=pl.ANY)
+    near = pl.BlockSpec(memory_space=pltpu.VMEM)
     return pl.pallas_call(
         backward_kernel,
         name="backward",
-        grid=(F // FB,),
-        in_specs=[
-            SMEM, SMEM, whole(ROWS, F, 128), cols_at(F), rows_at(PAIRS), rows_at(ROWS),
-            rows_at(ROWS), rows_at(ROWS), whole(16, 144, 256), cols_at(80), cols_at(256),
-            cols_at(9), whole(2, 128, 256), whole(512, 128), cols_at(F), cols_at(256),
-            whole(3 * F + 48, 128), whole(2, CH, 128),
-        ],
-        out_specs=[whole(HALF_ROWS, 128)] * 2,
+        in_specs=[SMEM, SMEM] + [far] * 4 + [near] * 12,
+        out_specs=[near] * 2,
         out_shape=[shaped(HALF_ROWS, 128, dtype=HALF)] * 2,
         scratch_shapes=[
-            pltpu.SMEM((2,), WIDE),
-            pltpu.VMEM((704, 128), HALF),
-            pltpu.VMEM((FB, 128), WIDE),
-            pltpu.VMEM((ROWS, FB, 128), WIDE),
-            pltpu.VMEM((ROWS, FB, 128), HALF),
+            *[pltpu.VMEM((ROWS, F, 128), HALF)] * 4,
+            pltpu.VMEM((2, HALF_ROWS, 128), HALF),
+            pltpu.VMEM((F, 128), WIDE),
+            pltpu.VMEM((F, F), WIDE),
+            pltpu.VMEM((ROWS, F, 128), HALF),
+            pltpu.VMEM((ROWS, F, 128), HALF),
+            pltpu.SemaphoreType.DMA((28,)),
         ],
-        compiler_params=params(("arbitrary",)),
+        compiler_params=params(),
         cost_estimate=pl.CostEstimate(flops=3 * 10**9, bytes_accessed=16 * 10**6, transcendentals=0),
     )(
-        core, coef, cotan, point, quarter_back, act, steep, depth, maps, lat_fine, lat_coarse,
-        kern, jnp.asarray(upsampler_rows(), HALF), jnp.asarray(pooler(1.0), HALF), part_point,
-        part_lat, packed_coarse, sums_coarse,
+        core, coef, cotan, act, steep, depth, point, quarter_back, maps, lat_fine, lat_coarse, kern,
+        jnp.asarray(upsampler_rows(), HALF), jnp.asarray(pooler(1.0), HALF), part_point, part_lat,
+        packed_coarse, sums_coarse,
     )
 
 
@@ -509,21 +548,30 @@
 
 
 def to_images(values):
-    return lax.all_to_all(values, "space", split_axis=0, concat_axis=0, tiled=True)
+    return lax.all_to_all(values, SPACE, split_axis=0, concat_axis=0, tiled=True)
 
 
 def to_other_core(values):
     return lax.ppermute(values, "core", [(0, 1), (1, 0)])
 
 
+def to_all(values, axes):
+    count = lax.axis_size(axes)
+    copies = lax.optimization_barrier(jnp.broadcast_to(values[None], (count,) + values.shape))
+    return lax.all_to_all(copies, axes, 0, 0, tiled=True)
+
+
+def added(values):
+    return lax.optimization_barrier(jnp.sum(values.astype(WIDE), axis=0)).astype(HALF)
+
+
 def sum_over_devices(keep, send):
-    count = lax.axis_size("group") * lax.axis_size("space")
-    share = HALF_ROWS // (2 * count)
+    count = lax.axis_size(LEVEL)
     both = (keep.astype(WIDE) + to_other_core(send).astype(WIDE)).astype(HALF)
-    mine = lax.all_to_all(both.reshape(count, share, 2, 128), CHIPS, 0, 0, tiled=True)
-    mine = lax.optimization_barrier(jnp.sum(mine.astype(WIDE), axis=0)).astype(HALF)
-    mine = lax.optimization_barrier(jnp.broadcast_to(mine[None], (count,) + mine.shape))
-    mine = lax.all_to_all(mine, CHIPS, 0, 0, tiled=True).reshape(HALF_ROWS, 128)
+    shares = both.reshape(count, HALF_ROWS // count, 128)
+    mine = added(lax.all_to_all(shares, LEVEL, 0, 0, tiled=True))
+    mine = added(to_all(mine, "z"))
+    mine = to_all(mine, LEVEL).reshape(HALF_ROWS, 128)
     return mine, to_other_core(mine)
 
 
@@ -545,9 +593,8 @@
     ratio = joining / jnp.stack([fine_total, fine_total, coarse_total, coarse_total])
     coef = jnp.concatenate([ratio, jnp.stack([1.0 / fine_total, 1.0 / coarse_total])])
     core = lax.axis_index("core").astype(jnp.int32)[None]
-    fine = fine_map.reshape(16, 80, 256)
     coarse = jnp.transpose(coarse_map, (0, 2, 3, 1)).reshape(16, 64, 224)
-    maps = to_images(jnp.concatenate([fine, jnp.pad(coarse, ((0, 0), (0, 0), (0, 32)))], axis=1))
+    maps = to_images(join_maps(fine_map, coarse))
     cotan = with_layout_constraint(jnp.transpose(fine_cotan, (0, 2, 1, 3)), ROW_MAJOR)
     maps, cotan = lax.optimization_barrier((maps, cotan))
     cotan = to_images(cotan).reshape(ROWS, F, 128)
@@ -572,16 +619,16 @@
 
 def solution(mesh):
     dp, space = mesh.devices.shape
-    finer = Mesh(mesh.devices.reshape(dp // 2, 2, space), ("group", "core", "space"))
+    finer = Mesh(mesh.devices.reshape(dp // 2, 2, space // 2, 2), ("group", "core", "z", "y"))
     dp = ("group", "core")
     return jax.shard_map(
         body,
         mesh=finer,
         in_specs=(
-            P(dp, None, "space", None),
-            P(dp, None, "space", None),
-            P(dp, None, "space", None),
-            P((*dp, "space"), None, None, None),
+            P(dp, None, SPACE, None),
+            P(dp, None, SPACE, None),
+            P(dp, None, SPACE, None),
+            P((*dp, *SPACE), None, None, None),
             P(),
             P(),
             P(),

time: 210 us -> 195 us (0.929)
  blocking collectives: 50.1 us -> 40.1 us
  Pallas kernels: 58.4 us -> 55.8 us
  other arithmetic: 2.89 us -> 0.38 us
    all_to_all x2 -> x3, blocking collectives: 50.1 us -> 40.1 us  [the longest x2 24 us: to_all(): return lax.all_to_all(copies, axes, 0, 0, tiled=True)]
    unnamed x30 -> x34, local copies, waits for them, and re-layouts: 6.64 us -> 9.73 us
    pallas_call x1 -> x2, Pallas kernels: 25 us -> 22.3 us  [the longest x1 20.3 us: backward(): pl.pallas_call(backward_kernel, name='backward', in_specs=[SMEM, SMEM] +...]
    reshape x1 -> x0, local copies, waits for them, and re-layouts: 2.22 us -> none  [body(): fine = fine_map.reshape(16, 80, 256)]
    concatenate x1 -> x0, other arithmetic: 2.19 us -> none  [body(): jnp.concatenate([fine, jnp.pad(coarse, ((0, 0), (0, 0), (0, 32)))], axis=1)]
  transfers between devices with their start and end apart: 4 -> 4, of which waited for: 4 -> 4; matrix products, arithmetic and copies ran while one was open for 3% -> 3% of each run, Pallas kernels for 15% -> 17%
where the time goes in v3:
time: 195 us
  waiting for transfers between devices  59.5 us (31%)
  Pallas kernels  55.8 us (29%)
  blocking collectives  40.1 us (21%)
  starting transfers between devices  24.1 us (12%)
  local copies, waits for them, and re-layouts  11.3 us (6%)
  between operations  3.55 us (2%)
    all_to_all x2, waiting for transfers between devices, to_images(): lax.all_to_all(values, SPACE, split_axis=0, concat_axis=0, tiled=True)  56.6 us
    all_to_all x2, blocking collectives, to_all(): return lax.all_to_all(copies, axes, 0, 0, tiled=True)  24 us
    pallas_call x1, Pallas kernels, backward(): pl.pallas_call(backward_kernel, name='backward', in_specs=[SMEM, SMEM] +...  20.3 us
    pallas_call x1, Pallas kernels, coarse_node(): pl.pallas_call(coarse_kernel, name='coarse_node', in_specs=[SMEM] + [pl.B...  18.7 us
    all_to_all x2, starting transfers between devices, to_images(): lax.all_to_all(values, SPACE, split_axis=0, concat_axis=0, tiled=True)  17.2 us
    all_to_all x1, blocking collectives, sum_over_devices(): mine = added(lax.all_to_all(shares, LEVEL, 0, 0, tiled=True))  16.1 us
    pallas_call x1, Pallas kernels, forward(): pl.pallas_call(forward_kernel, name='forward', grid=(F // FB,), in_specs=...  13.5 us
    unnamed x34, local copies, waits for them, and re-layouts  9.73 us
  transfers between devices with their start and end apart: 4, of which 4 were waited for; matrix products, arithmetic and copies ran while one was open for 3% of the time, Pallas kernels for 17%

profile of v3, /device:TPU:1, one launch (start us, length us, event | category | flops | bytes accessed | tf_op | source)
XLA Modules:
  0.0 194.6 jit_solution(3932334527462799330)
XLA Ops:
  0.6 0.0 copy-start.3
  0.6 1.1 copy-done.3
  1.7 1.0 copy-done.4
  2.8 2.0 %join_maps.1 = bf16[16,144,256]{2,1,0:T(8,128)(2,1)} custom-call(bf16[16,80,2,128]{3,2,1,0:T(2,128)(2,1)S(1)} %copy-done.3, bf16[16,64,224]{2,1,0:T(8,128)(2,1)S(1)} %bitcast.28), custom_call_target="tpu_custom_call" | custom-call | tf_op jit(solution)/shard_map/join_maps/pallas_call | solution.py:417
  4.7 10.1 %all-to-all-start = ((bf16[16,144,256]{2,1,0:T(8,128)(2,1)}), bf16[16,144,256]{2,1,0:T(8,128)(2,1)S(1)}, u32[]{:S(2)}, u32[]{:S(2)}) async-start(bf16[16,144,256]{2,1,0:T(8,128)(2,1)} %join_maps.1), calls=%async_computation | async-start | bytes 2359296 | tf_op jit(solution)/shard_map/all_to_all | solution.py:551
  14.9 4.3 %copy.44 = bf16[16,384,2,128]{3,1,2,0:T(8,128)(2,1)} copy(bf16[16,384,2,128]{3,2,1,0:T(2,128)(2,1)} %param.17) | data formatting | bytes 6291456 | tf_op args[2]
  19.2 23.3 %all-to-all-done.maps = bf16[16,144,256]{2,1,0:T(8,128)(2,1)S(1)} async-done(((bf16[16,144,256]{2,1,0:T(8,128)(2,1)}), bf16[16,144,256]{2,1,0:T(8,128)(2,1)S(1)}, u32[]{:S(2)}, u32[]{:S(2)}) %all-to-all-start) | async-done | bytes 1179680 | tf_op jit(solution)/shard_map/all_to_all | solution.py:551
  42.4 0.0 copy-start.11
  42.5 0.0 copy-start.10
  42.5 0.0 copy-start.1
  42.5 0.0 copy-start.8
  42.5 0.0 copy-start.9
  42.5 7.1 %all-to-all-start.1 = ((bf16[16,2,384,128]{3,2,1,0:T(8,128)(2,1)}), bf16[16,2,384,128]{3,2,1,0:T(8,128)(2,1)}, u32[]{:S(2)}, u32[]{:S(2)}) async-start(bf16[16,2,384,128]{3,2,1,0:T(8,128)(2,1)} %bitcast.31), calls=%async_computation.1 | async-start | bytes 6291456 | tf_op jit(solution)/shard_map/all_to_all | solution.py:551
  49.6 0.0 copy-done.14
  49.6 0.6 fusion
  52.9 0.0 copy-done.12
  52.9 0.0 copy-done.13
  52.9 0.0 copy-done.11
  52.9 0.1 copy.38
  53.1 0.1 copy.42
  53.2 0.1 copy.40
  53.4 0.1 copy.39
  53.5 0.0 copy-done.1
  53.5 0.2 copy.41
  53.8 0.1 maximum_divide_fusion
  53.9 0.1 pad_maximum_fusion.coef
  54.0 0.0 copy-done.9
  54.0 0.0 copy-start.6
  54.0 13.5 %forward.1 = (bf16[32,384,128]{2,1,0:T(8,128)(2,1)}, bf16[32,384,128]{2,1,0:T(8,128)(2,1)}, bf16[32,384,128]{2,1,0:T(8,128)(2,1)}, bf16[8,384,128]{2,1,0:T(8,128)(2,1)S(1)}, bf16[8,384,128]{2,1,0:T(8,128)(2,1)S(1)}) custom-call(f32[6]{0:T(128)S(1)} %pad_maximum_fusion.coef, bf16[16,144,256]{2,1,0:T(8,128)(2,1)S(1)} %all-to-all-done.maps, ...), custom_call_target="tpu_custom_call" | custom-call | flops 1000000000 | bytes 12000000 | tf_op jit(solution)/shard_map/forward/pallas_call | solution.py:432
  67.5 0.9 copy-done.2
  68.4 1.0 copy-done.5
  69.3 18.7 %coarse_node.1 = (bf16[1200,128]{1,0:T(8,128)(2,1)S(1)}, f32[384,384]{1,0:T(8,128)S(1)}, bf16[8,384,128]{2,1,0:T(8,128)(2,1)S(1)}, f32[384,256]{1,0:T(8,128)S(1)}, f32[2,16,128]{2,1,0:T(8,128)S(1)}) custom-call(f32[6]{0:T(128)S(1)} %pad_maximum_fusion.coef, bf16[8,384,128]{2,1,0:T(8,128)(2,1)S(1)} %get-tuple-element.33.pooled_depth, ...), custom_call_target="tpu_custom_call" | custom-call | flops 1000000000 | bytes 5000000 | tf_op jit(solution)/shard_map/coarse_node/pallas_call | solution.py:455
  88.1 33.4 %all-to-all-done.1 = bf16[16,2,384,128]{3,2,1,0:T(8,128)(2,1)} async-done(((bf16[16,2,384,128]{3,2,1,0:T(8,128)(2,1)}), bf16[16,2,384,128]{3,2,1,0:T(8,128)(2,1)}, u32[]{:S(2)}, u32[]{:S(2)}) %all-to-all-start.1) | async-done | bytes 3145760 | tf_op jit(solution)/shard_map/all_to_all | solution.py:551
  121.4 0.0 copy-done.6
  121.4 0.9 copy-done.7
  122.3 20.3 %backward.1 = (bf16[1792,128]{1,0:T(8,128)(2,1)S(1)}, bf16[1792,128]{1,0:T(8,128)(2,1)S(1)}) custom-call(s32[1]{0:T(128)} %bitcast.core, f32[6]{0:T(128)S(1)} %pad_maximum_fusion.coef, bf16[32,384,128]{2,1,0:T(8,128)(2,1)} %bitcast.5.cotan_far, bf16[32,384,128]{2,1,0:T(8,128)(2,1)} %get-tuple-element.30.act_far, ...), custom_call_target="tpu_custom_call" | custom-call | flops 3000000000 | bytes 16000000 | tf_op jit(solution)/shard_map/backward/pallas_call | solution.py:481
  142.7 2.3 %collective-permute-start = (bf16[1792,128]{1,0:T(8,128)(2,1)S(1)}, bf16[1792,128]{1,0:T(8,128)(2,1)S(1)}, u32[]{:S(2)}, u32[]{:S(2)}) collective-permute-start(bf16[1792,128]{1,0:T(8,128)(2,1)S(1)} %get-tuple-element.41), channel_id=1, source_target_pairs={{0,16},{16,0},{1,17},{17,1},{2,18},{18,2},{3,19},{19,3},{4,20},{20... | collective-permute-start | bytes 1376264 | tf_op jit(solution)/shard_map/ppermute | solution.py:555
  144.9 1.4 collective-permute-done
  146.4 0.1 add_convert_fusion
  146.5 16.1 %all_to_all.25 = bf16[16,112,128]{2,1,0:T(8,128)(2,1)S(1)} all-to-all(bf16[16,112,128]{2,1,0:T(8,128)(2,1)S(1)} %bitcast.32), channel_id=1, replica_groups=mesh['group'=8,'core'=2,'z'=8,'y'=2] {'group','y'}, dimensions={0} | all-to-all | bytes 917504 | tf_op jit(solution)/shard_map/all_to_all | solution.py:572
  162.6 0.1 convert_reduce_fusion
  162.7 12.1 %all_to_all.26 = bf16[8,112,128]{2,1,0:T(8,128)(2,1)S(1)} all-to-all(bf16[8,112,128]{2,1,0:T(8,128)(2,1)S(1)} %broadcast_in_dim.7), channel_id=1, replica_groups=mesh['group'=8,'core'=2,'z'=8,'y'=2] {'z'}, dimensions={0} | all-to-all | bytes 458752 | tf_op jit(solution)/shard_map/all_to_all | solution.py:561
  174.9 0.1 broadcast_in_dim.8
  174.9 11.8 %all_to_all.27 = bf16[16,112,128]{2,1,0:T(8,128)(2,1)S(1)} all-to-all(bf16[16,112,128]{2,1,0:T(8,128)(2,1)S(1)} %broadcast_in_dim.8), channel_id=1, replica_groups=mesh['group'=8,'core'=2,'z'=8,'y'=2] {'group','y'}, dimensions={0} | all-to-all | bytes 917504 | tf_op jit(solution)/shard_map/all_to_all | solution.py:561
  186.8 4.6 %collective-permute-start.1 = (bf16[1792,128]{1,0:T(8,128)(2,1)S(1)}, bf16[1792,128]{1,0:T(8,128)(2,1)S(1)}, u32[]{:S(2)}, u32[]{:S(2)}) collective-permute-start(bf16[1792,128]{1,0:T(8,128)(2,1)S(1)} %bitcast.22), channel_id=1, source_target_pairs={{0,16},{16,0},{1,17},{17,1},{2,18},{18,2},{3,19},{19,3},{4,20},{20... | collective-permute-start | bytes 1376264 | tf_op jit(solution)/shard_map/ppermute | solution.py:555
  191.4 1.4 collective-permute-done.1.other
  192.8 1.3 unpack.1
  194.1 0.5 slice_bitcast_fusion
  (16 shorter events, 0.1 us)
Async XLA Ops:
  0.6 1.1 copy-start.3
  1.7 1.0 copy-start.4
  4.7 37.7 %all-to-all-start = ((bf16[16,144,256]{2,1,0:T(8,128)(2,1)}), bf16[16,144,256]{2,1,0:T(8,128)(2,1)S(1)}, u32[]{:S(2)}, u32[]{:S(2)}) async-start(bf16[16,144,256]{2,1,0:T(8,128)(2,1)} %join_maps.1), calls=%async_computation | async-start | bytes 2359296 | tf_op jit(solution)/shard_map/all_to_all | solution.py:551
  42.4 11.5 %copy-start = (bf16[16,144,256]{2,1,0:T(8,128)(2,1)}, bf16[16,144,256]{2,1,0:T(8,128)(2,1)S(1)}, u32[]{:S(2)}) copy-start(bf16[16,144,256]{2,1,0:T(8,128)(2,1)S(1)} %all-to-all-done.maps) | copy-start | bytes 3538948
  42.4 7.2 %copy-start.14 = (f32[4]{0:T(128)S(1)}, f32[4]{0:T(128)}, u32[]{:S(2)}) copy-start(f32[4]{0:T(128)} %param.25) | copy-start | bytes 52
  42.4 10.4 %copy-start.12 = (f32[3,3,384]{2,1,0:T(4,128)S(1)}, f32[3,3,384]{2,1,0:T(4,128)}, u32[]{:S(2)}) copy-start(f32[3,3,384]{2,1,0:T(4,128)} %param.23) | copy-start | bytes 41476
  42.4 10.5 %copy-start.13 = (f32[3,3,384]{2,1,0:T(4,128)S(1)}, f32[3,3,384]{2,1,0:T(4,128)}, u32[]{:S(2)}) copy-start(f32[3,3,384]{2,1,0:T(4,128)} %param.24) | copy-start | bytes 41476
  42.4 10.5 %copy-start.11 = (bf16[80,384]{1,0:T(8,128)(2,1)S(1)}, bf16[80,384]{1,0:T(8,128)(2,1)}, u32[]{:S(2)}) copy-start(bf16[80,384]{1,0:T(8,128)(2,1)} %param.19) | copy-start | bytes 184324
  42.5 10.9 %copy-start.10 = (bf16[224,384]{1,0:T(8,128)(2,1)S(1)}, bf16[224,384]{1,0:T(8,128)(2,1)}, u32[]{:S(2)}) copy-start(bf16[224,384]{1,0:T(8,128)(2,1)} %param.20) | copy-start | bytes 516100
  42.5 11.1 %copy-start.1 = (bf16[384,384]{1,0:T(8,128)(2,1)S(1)}, bf16[384,384]{1,0:T(8,128)(2,1)}, u32[]{:S(2)}) copy-start(bf16[384,384]{1,0:T(8,128)(2,1)} %point.1) | copy-start | bytes 884740
  42.5 11.5 %copy-start.8 = (bf16[512,128]{1,0:T(8,128)(2,1)S(1)}, bf16[512,128]{1,0:T(8,128)(2,1)}, u32[]{:S(2)}) copy-start(bf16[512,128]{1,0:T(8,128)(2,1)} %constant.28.clone.pool) | copy-start | bytes 393220
  42.5 11.5 %copy-start.9 = (bf16[128,256]{1,0:T(8,128)(2,1)S(1)}, bf16[128,256]{1,0:T(8,128)(2,1)}, u32[]{:S(2)}) copy-start(bf16[128,256]{1,0:T(8,128)(2,1)} %constant.27.clone.up) | copy-start | bytes 196612
  42.5 78.9 %all-to-all-start.1 = ((bf16[16,2,384,128]{3,2,1,0:T(8,128)(2,1)}), bf16[16,2,384,128]{3,2,1,0:T(8,128)(2,1)}, u32[]{:S(2)}, u32[]{:S(2)}) async-start(bf16[16,2,384,128]{3,2,1,0:T(8,128)(2,1)} %bitcast.31), calls=%async_computation.1 | async-start | bytes 6291456 | tf_op jit(solution)/shard_map/all_to_all | solution.py:551
  54.0 67.4 %copy-start.6 = (bf16[512,128]{1,0:T(8,128)(2,1)S(1)}, bf16[512,128]{1,0:T(8,128)(2,1)}, u32[]{:S(2)}) copy-start(bf16[512,128]{1,0:T(8,128)(2,1)} %constant.30.clone.pool) | copy-start | bytes 393220
  67.5 0.9 copy-start.2
  68.4 1.0 copy-start.5
  121.4 0.9 copy-start.7
  142.7 3.7 %collective-permute-start = (bf16[1792,128]{1,0:T(8,128)(2,1)S(1)}, bf16[1792,128]{1,0:T(8,128)(2,1)S(1)}, u32[]{:S(2)}, u32[]{:S(2)}) collective-permute-start(bf16[1792,128]{1,0:T(8,128)(2,1)S(1)} %get-tuple-element.41), channel_id=1, source_target_pairs={{0,16},{16,0},{1,17},{17,1},{2,18},{18,2},{3,19},{19,3},{4,20},{20... | collective-permute-start | bytes 1376264 | tf_op jit(solution)/shard_map/ppermute | solution.py:555
  186.8 6.0 %collective-permute-start.1 = (bf16[1792,128]{1,0:T(8,128)(2,1)S(1)}, bf16[1792,128]{1,0:T(8,128)(2,1)S(1)}, u32[]{:S(2)}, u32[]{:S(2)}) collective-permute-start(bf16[1792,128]{1,0:T(8,128)(2,1)S(1)} %bitcast.22), channel_id=1, source_target_pairs={{0,16},{16,0},{1,17},{17,1},{2,18},{18,2},{3,19},{19,3},{4,20},{20... | collective-permute-start | bytes 1376264 | tf_op jit(solution)/shard_map/ppermute | solution.py:555

commit v4 on v3

--- a/solution.py
+++ b/solution.py
@@ -1,6 +1,5 @@
 import jax
 import jax.numpy as jnp
-import numpy as np
 from jax import lax
 from jax.experimental.layout import Layout, with_layout_constraint
 from jax.experimental import pallas as pl
@@ -30,30 +29,23 @@
     return lax.dot_general(left, right, (((1,), (1,)), ((), ())), preferred_element_type=WIDE)
 
 
-def upsampler():
-    out = np.zeros((128, 256), np.float32)
-    for col in range(128):
-        out[col, 2 * col] = 1.0
-        out[col, 2 * col + 1] = 1.0
-    return out
-
-
-def upsampler_rows():
-    one = upsampler()
-    out = np.zeros((2, 128, 256), np.float32)
-    for odd in range(2):
-        half = one[:, 128 * odd : 128 * odd + 128]
-        out[odd, :, :128] = half
-        out[odd, :, 128:] = half
-    return out
-
-
-def pooler(scale):
-    one = upsampler()
-    out = np.zeros((512, 128), np.float32)
-    for row in range(4):
-        out[128 * row : 128 * row + 128] = one[:, 128 * (row // 2) : 128 * (row // 2) + 128].T
-    return out * scale
+def ones_where(condition):
+    return jnp.where(condition, 1.0, 0.0).astype(HALF)
+
+
+def upsampler(rows):
+    shape = (128, 256)
+    cell = lax.broadcasted_iota(jnp.int32, shape, 0)
+    lane = lax.broadcasted_iota(jnp.int32, shape, 1)
+    row = jnp.where(lane < 128, rows[0], rows[1])
+    return ones_where(cell == 64 * row + ((lane & 127) >> 1))
+
+
+def pooler():
+    shape = (512, 128)
+    cell = lax.broadcasted_iota(jnp.int32, shape, 0)
+    lane = lax.broadcasted_iota(jnp.int32, shape, 1)
+    return ones_where(lane == ((cell >> 8) << 6) + ((cell & 127) >> 1))
 
 
 def lanes(shape):
@@ -98,8 +90,20 @@
     return jnp.concatenate([maps[2 * k, 80:144], maps[2 * k + 1, 80:144]], axis=0)
 
 
-def join_kernel(fine, coarse, maps):
-    for i in range(maps.shape[0]):
+def join_kernel(fine_far, coarse_far, maps, fine, coarse, arrived):
+    count = maps.shape[0]
+    step = count // 8
+    copies = []
+    for q in range(8):
+        at = pl.ds(step * q, step)
+        copies.append(pltpu.make_async_copy(fine_far.at[at], fine.at[at], arrived.at[q]))
+        copies.append(pltpu.make_async_copy(coarse_far.at[at], coarse.at[at], arrived.at[8 + q]))
+    for copy in copies:
+        copy.start()
+    for i in range(count):
+        if i % step == 0:
+            copies[2 * i // step].wait()
+            copies[2 * i // step + 1].wait()
         maps[i, :80] = fine[i].reshape(80, 256)
         maps[i, 80:, :128] = coarse[i, :, :128]
         maps[i, 80:, 128:224] = coarse[i, :, 128:]
@@ -107,13 +111,14 @@
 
 
 def forward_kernel(
-    coef, maps, lat_fine, lat_coarse, kern, up, pool,
-    act_out, slope_out, depth_out, proj_out, pooled_out, proj, lifted,
+    coef, maps, lat_fine, lat_coarse, kern,
+    act_out, slope_out, turned_out, proj_out, pooled_out, proj, lifted, depth,
 ):
+    up, pool = upsampler((0, 1)), pooler()
     for k in range(PAIRS):
         pair = nt(lat_coarse[...], coarse_pair(maps, k)).astype(HALF)
         proj_out[k] = pair
-        both = nn(pair, up[...])
+        both = nn(pair, up)
         lifted[2 * k] = both[:, :128]
         lifted[2 * k + 1] = both[:, 128:]
     for s in range(ROWS // 2):
@@ -145,12 +150,14 @@
                     for v in range(3):
                         term = taps[u][v] * sides[r - 2 + u][v]
                         total = term if total is None else total + term
-                depth_out[r - 1, at, :] = total.astype(HALF)
+                depth[r - 1, at, :] = total.astype(HALF)
                 sides.pop(r - 2, None)
 
     for k in range(PAIRS):
-        four = jnp.concatenate([depth_out[4 * k + a] for a in range(4)], axis=1)
-        pooled_out[k] = nn(four, pool[...]).astype(HALF)
+        four = jnp.concatenate([depth[4 * k + a] for a in range(4)], axis=1)
+        pooled_out[k] = (0.25 * nn(four, pool)).astype(HALF)
+    for r in range(ROWS):
+        turned_out[128 * r : 128 * r + 128] = depth[r].T
 
 
 def coarse_kernel(
@@ -234,7 +241,7 @@
     point, point_f, lat = None, None, None
     for k in range(PAIRS):
         point = accumulate(point, nn(depth_s[k], cotan[k]))
-        point_f = accumulate(point_f, nt(pooled_depth[k], pooled_back[k]))
+        point_f = accumulate(point_f, nt(pooled_back[k], pooled_depth[k]))
         lat = accumulate(lat, nn(own_back[k], coarse_pair(maps, k)))
         quarter_back[k] = (0.25 * nn(point_fine[...], pooled_back[k])).astype(HALF)
     for j in range(F // 128):
@@ -246,12 +253,12 @@
 
 
 def backward_kernel(
-    core, coef, cotan_far, act_far, steep_far, depth_far, point, quarter_back, maps, lat_fine,
-    lat_coarse, kern, up, pool, part_point, part_lat, packed_coarse, sums_coarse,
+    core, coef, cotan_far, act_far, steep_far, depth_far, maps_far, point, quarter_back, lat_fine,
+    lat_coarse, kern, part_point, part_lat, packed_coarse, sums_coarse,
     keep, send,
-    cotan, act, steep, depth, halves, grad_kern, grad_point, back, slope_s, arrived,
+    cotan, act, steep, depth, maps, halves, grad_kern, grad_point, back, slope_s, arrived,
 ):
-    quarter = ROWS // 4
+    quarter = ROWS // 8
     share = F // PAIRS
 
     def of_cotan(q):
@@ -260,24 +267,27 @@
 
     def of_step(step):
         at = pl.ds(pl.multiple_of(share * step, 16), share)
-        rows = pl.ds(4 * step, 4)
+        rows = pl.ds(pl.multiple_of(512 * step, 512), 512)
         return [
-            pltpu.make_async_copy(act_far.at[:, at], act.at[:, at], arrived.at[4 + step]),
-            pltpu.make_async_copy(steep_far.at[:, at], steep.at[:, at], arrived.at[12 + step]),
-            pltpu.make_async_copy(depth_far.at[rows], depth.at[rows], arrived.at[20 + step]),
+            pltpu.make_async_copy(act_far.at[:, at], act.at[:, at], arrived.at[8 + step]),
+            pltpu.make_async_copy(steep_far.at[:, at], steep.at[:, at], arrived.at[16 + step]),
+            pltpu.make_async_copy(depth_far.at[rows], depth.at[rows], arrived.at[24 + step]),
         ]
 
-    for q in range(4):
+    for q in range(8):
         of_cotan(q).start()
     for step in range(PAIRS):
         for copy in of_step(step):
             copy.start()
+    of_maps = pltpu.make_async_copy(maps_far, maps, arrived.at[32])
+    of_maps.start()
     grad_kern[...] = jnp.zeros_like(grad_kern)
     grad_point[...] = part_point[...]
     halves[0, 1408:] = packed_coarse[:F]
     halves[1, 704:1520] = packed_coarse[F:]
     halves[1, 1536:] = jnp.zeros((256, 128), HALF)
 
+    up, pool = [upsampler((odd, odd)) for odd in range(2)], pooler()
     for s in range(ROWS // 2):
         if 2 * s % quarter == 0:
             of_cotan(2 * s // quarter).wait()
@@ -294,9 +304,9 @@
     def _(step):
         for copy in of_step(step):
             copy.wait()
-        grad_point[...] += nt(
-            jnp.concatenate([depth[4 * step + a] for a in range(4)], axis=1),
+        grad_point[...] += nn(
             jnp.concatenate([cotan[4 * step + a] for a in range(4)], axis=1),
+            depth[pl.ds(pl.multiple_of(512 * step, 512), 512)],
         )
         lane = lanes((CH, 128))
         first_lane, last_lane = lane == 0, lane == 127
@@ -308,26 +318,30 @@
                 for left, middle, right in taps_of(kern, start)
             ]
             weight = [[None] * 3 for _ in range(3)]
-            sides = {}
+            totals, actives = {}, {}
             for r in range(ROWS + 1):
                 if r < ROWS:
-                    cells = back[r, at, :]
+                    actives[r] = act[r, at, :].astype(WIDE)
+                if r >= 1:
+                    q = r - 1
+                    cells = back[q, at, :]
                     turned = (pltpu.roll(cells, 127, 1), cells, pltpu.roll(cells, 1, 1))
-                    sides[r] = [c.astype(WIDE) for c in turned]
-                if r >= 1:
-                    active = act[r - 1, at, :].astype(WIDE)
-                    total = None
+                    near = [c.astype(WIDE) for c in turned]
                     for u in range(3):
-                        if r - u not in sides:
+                        i = q - 1 + u
+                        if i not in actives:
                             continue
                         for v in range(3):
-                            shifted = sides[r - u][v]
-                            term = taps[u][v] * shifted
-                            total = term if total is None else total + term
-                            more = active * shifted
+                            term = taps[u][v] * near[v]
+                            totals[i] = term if i not in totals else totals[i] + term
+                            more = actives[i] * near[v]
                             weight[u][v] = more if weight[u][v] is None else weight[u][v] + more
-                    slope_s[r - 1, at, :] = (total * steep[r - 1, at, :].astype(WIDE)).astype(HALF)
-                    sides.pop(r - 2, None)
+                    done = [q - 1] if r < ROWS else [q - 1, q]
+                    for i in done:
+                        if i >= 0:
+                            gate = steep[i, at, :].astype(WIDE)
+                            slope_s[i, at, :] = (totals.pop(i) * gate).astype(HALF)
+                            actives.pop(i)
             for u in range(3):
                 cleared = [
                     jnp.where(last_lane, 0.0, weight[u][0]),
@@ -340,13 +354,14 @@
     def accumulate(total, term):
         return term if total is None else total + term
 
+    of_maps.wait()
     lat_f, lat_c = None, None
     for k in range(PAIRS):
         four = jnp.concatenate([slope_s[4 * k + a] for a in range(4)], axis=1)
         both = jnp.concatenate([fine_pair(maps, 2 * k), fine_pair(maps, 2 * k + 1)], axis=1)
         lat_f = accumulate(lat_f, nt(four, both))
-        lat_c = accumulate(lat_c, nn(nn(four, pool[...]).astype(HALF), coarse_pair(maps, k)))
-    point_t = grad_point[...].astype(HALF)
+        lat_c = accumulate(lat_c, nn(nn(four, pool).astype(HALF), coarse_pair(maps, k)))
+    point_t = grad_point[...].T.astype(HALF)
     wide_f = jnp.concatenate([coef[0] * lat_f, jnp.zeros((F, 48), WIDE)], axis=1)
     lat_f_t = wide_f.T[:80].astype(HALF)
     lat_c_t = (coef[1] * lat_c + part_lat[...]).T[:224].astype(HALF)
@@ -413,18 +428,18 @@
 
 
 def join_maps(fine, coarse):
-    step = 4
     return pl.pallas_call(
         join_kernel,
         name="join_maps",
-        grid=(16 // step,),
-        in_specs=[
-            pl.BlockSpec((step, 80, 2, 128), lambda i: (i, 0, 0, 0)),
-            pl.BlockSpec((step, 64, 224), lambda i: (i, 0, 0)),
+        in_specs=[pl.BlockSpec(memory_space=pl.ANY)] * 2,
+        out_specs=pl.BlockSpec(memory_space=pltpu.VMEM),
+        out_shape=shaped(16, 144, 256, dtype=HALF),
+        scratch_shapes=[
+            pltpu.VMEM((16, 80, 2, 128), HALF),
+            pltpu.VMEM((16, 64, 224), HALF),
+            pltpu.SemaphoreType.DMA((16,)),
         ],
-        out_specs=pl.BlockSpec((step, 144, 256), lambda i: (i, 0, 0)),
-        out_shape=shaped(16, 144, 256, dtype=HALF),
-        compiler_params=params(("arbitrary",)),
+        compiler_params=pltpu.CompilerParams(vmem_limit_bytes=60 * 1024 * 1024),
     )(fine, coarse)
 
 
@@ -434,20 +449,24 @@
         name="forward",
         grid=(F // FB,),
         in_specs=[
-            SMEM, whole(16, 144, 256), cols_at(80), cols_at(256), cols_at(9), whole(128, 256),
-            whole(512, 128),
+            SMEM, whole(16, 144, 256), cols_at(80), cols_at(256), cols_at(9),
         ],
-        out_specs=[rows_at(ROWS), rows_at(ROWS), rows_at(ROWS), rows_at(PAIRS), rows_at(PAIRS)],
-        out_shape=[shaped(ROWS, F, 128, dtype=HALF)] * 3 + [shaped(PAIRS, F, 128, dtype=HALF)] * 2,
+        out_specs=[
+            rows_at(ROWS), rows_at(ROWS), pl.BlockSpec((ROWS * 128, FB), lambda j: (0, j)),
+            rows_at(PAIRS), rows_at(PAIRS),
+        ],
+        out_shape=[shaped(ROWS, F, 128, dtype=HALF)] * 2
+        + [shaped(ROWS * 128, F, dtype=HALF)]
+        + [shaped(PAIRS, F, 128, dtype=HALF)] * 2,
         scratch_shapes=[
             pltpu.VMEM((ROWS, FB, 128), WIDE),
             pltpu.VMEM((ROWS // 2, FB, 128), WIDE),
+            pltpu.VMEM((ROWS, FB, 128), HALF),
         ],
         compiler_params=params(("arbitrary",)),
         cost_estimate=pl.CostEstimate(flops=10**9, bytes_accessed=12 * 10**6, transcendentals=10**6),
     )(
         coef, maps, lat_fine, lat_coarse, kern,
-        jnp.asarray(upsampler(), HALF), jnp.asarray(pooler(0.25), HALF),
     )
 
 
@@ -481,24 +500,25 @@
     return pl.pallas_call(
         backward_kernel,
         name="backward",
-        in_specs=[SMEM, SMEM] + [far] * 4 + [near] * 12,
+        in_specs=[SMEM, SMEM] + [far] * 5 + [near] * 9,
         out_specs=[near] * 2,
         out_shape=[shaped(HALF_ROWS, 128, dtype=HALF)] * 2,
         scratch_shapes=[
-            *[pltpu.VMEM((ROWS, F, 128), HALF)] * 4,
+            *[pltpu.VMEM((ROWS, F, 128), HALF)] * 3,
+            pltpu.VMEM((ROWS * 128, F), HALF),
+            pltpu.VMEM((16, 144, 256), HALF),
             pltpu.VMEM((2, HALF_ROWS, 128), HALF),
             pltpu.VMEM((F, 128), WIDE),
             pltpu.VMEM((F, F), WIDE),
             pltpu.VMEM((ROWS, F, 128), HALF),
             pltpu.VMEM((ROWS, F, 128), HALF),
-            pltpu.SemaphoreType.DMA((28,)),
+            pltpu.SemaphoreType.DMA((33,)),
         ],
         compiler_params=params(),
         cost_estimate=pl.CostEstimate(flops=3 * 10**9, bytes_accessed=16 * 10**6, transcendentals=0),
     )(
-        core, coef, cotan, act, steep, depth, point, quarter_back, maps, lat_fine, lat_coarse, kern,
-        jnp.asarray(upsampler_rows(), HALF), jnp.asarray(pooler(1.0), HALF), part_point, part_lat,
-        packed_coarse, sums_coarse,
+        core, coef, cotan, act, steep, depth, maps, point, quarter_back, lat_fine, lat_coarse, kern,
+        part_point, part_lat, packed_coarse, sums_coarse,
     )
 
 
@@ -523,7 +543,10 @@
             rows, low = (halves[1], 704 + F * (j - 1)) if j else (halves[0], 1408)
             point_coarse[:, at] = rows[low : low + F].astype(WIDE)
         last = halves[1][1520:1536].astype(WIDE)
-        join[...] = (last + pltpu.roll(last, 124, 1) + pltpu.roll(last, 120, 1))[:8]
+        lane = lanes((16, 128))
+        first_row = lax.broadcasted_iota(jnp.int32, (16, 128), 0) == 0
+        for i in range(4):
+            join[i] = jnp.sum(jnp.where(first_row & ((lane & 3) == i) & (lane < 12), last, 0.0))
 
     @pl.when(core[0] == 0)
     def _():
@@ -541,8 +564,9 @@
         in_specs=[SMEM] + [pl.BlockSpec(memory_space=pltpu.VMEM)] * 2,
         out_shape=[
             shaped(80, F), shaped(224, F), shaped(F, F), shaped(F, F), shaped(3, 3, F),
-            shaped(3, 3, F), shaped(8, 128),
+            shaped(3, 3, F), shaped(4),
         ],
+        out_specs=[pl.BlockSpec(memory_space=pltpu.VMEM)] * 6 + [SMEM],
         compiler_params=params(),
     )(core, mine, other)
 
@@ -613,8 +637,7 @@
         core, coef, cotan, point_fine, quarter_back, act, steep, depth, maps, lat_fine,
         lat_coarse, kern_fine, part_point, part_lat, packed_coarse, sums_coarse,
     )
-    out = unpack(core, *sum_over_devices(keep, send))
-    return (*out[:6], out[6][0, :4])
+    return tuple(unpack(core, *sum_over_devices(keep, send)))
 
 
 def solution(mesh):

time: 195 us -> 192 us (0.985)
  local copies, waits for them, and re-layouts: 11.3 us -> 7.66 us
    unnamed x34 -> x22, local copies, waits for them, and re-layouts: 9.73 us -> 6.64 us
where the time goes in v4:
time: 192 us; the launch traced here: 191 us
  waiting for transfers between devices  59.6 us (31%)
  Pallas kernels  55.9 us (29%)
  blocking collectives  40.1 us (21%)
  starting transfers between devices  24.1 us (13%)
  local copies, waits for them, and re-layouts  7.66 us (4%)
  between operations  3.51 us (2%)
    all_to_all x2, waiting for transfers between devices, to_images(): lax.all_to_all(values, SPACE, split_axis=0, concat_axis=0, tiled=True)  56.7 us
    all_to_all x2, blocking collectives, to_all(): return lax.all_to_all(copies, axes, 0, 0, tiled=True)  24 us
    pallas_call x1, Pallas kernels, backward(): pl.pallas_call(backward_kernel, name='backward', in_specs=[SMEM, SMEM] +...  19.6 us
    pallas_call x1, Pallas kernels, coarse_node(): pl.pallas_call(coarse_kernel, name='coarse_node', in_specs=[SMEM] + [pl.B...  18.8 us
    all_to_all x2, starting transfers between devices, to_images(): lax.all_to_all(values, SPACE, split_axis=0, concat_axis=0, tiled=True)  17.2 us
    all_to_all x1, blocking collectives, sum_over_devices(): mine = added(lax.all_to_all(shares, LEVEL, 0, 0, tiled=True))  16.1 us
    pallas_call x1, Pallas kernels, forward(): pl.pallas_call(forward_kernel, name='forward', grid=(F // FB,), in_specs=...  13.4 us
    ppermute x2, starting transfers between devices, to_other_core(): return lax.ppermute(values, 'core', [(0, 1), (1, 0)])  6.87 us
  transfers between devices with their start and end apart: 4, of which 4 were waited for; matrix products, arithmetic and copies ran while one was open for 3% of the time, Pallas kernels for 17%

profile of v4, /device:TPU:1, one launch (start us, length us, event | category | flops | bytes accessed | tf_op | source)
XLA Modules:
  0.0 191.3 jit_solution(6447075018636418241)
XLA Ops:
  0.6 2.8 %join_maps.1 = bf16[16,144,256]{2,1,0:T(8,128)(2,1)} custom-call(bf16[16,80,2,128]{3,2,1,0:T(2,128)(2,1)} %fine_far.1, bf16[16,64,224]{2,1,0:T(8,128)(2,1)} %bitcast.32), custom_call_target="tpu_custom_call" | custom-call | tf_op jit(solution)/shard_map/join_maps/pallas_call | solution.py:431
  3.5 10.1 %all-to-all-start = ((bf16[16,144,256]{2,1,0:T(8,128)(2,1)}), bf16[16,144,256]{2,1,0:T(8,128)(2,1)S(1)}, u32[]{:S(2)}, u32[]{:S(2)}) async-start(bf16[16,144,256]{2,1,0:T(8,128)(2,1)} %join_maps.1), calls=%async_computation | async-start | bytes 2359296 | tf_op jit(solution)/shard_map/all_to_all | solution.py:575
  13.6 4.3 %copy.40 = bf16[16,384,2,128]{3,1,2,0:T(8,128)(2,1)} copy(bf16[16,384,2,128]{3,2,1,0:T(2,128)(2,1)} %param.13) | data formatting | bytes 6291456 | tf_op args[2]
  17.9 23.3 %all-to-all-done.maps.maps_far = bf16[16,144,256]{2,1,0:T(8,128)(2,1)S(1)} async-done(((bf16[16,144,256]{2,1,0:T(8,128)(2,1)}), bf16[16,144,256]{2,1,0:T(8,128)(2,1)S(1)}, u32[]{:S(2)}, u32[]{:S(2)}) %all-to-all-start) | async-done | bytes 1179680 | tf_op jit(solution)/shard_map/all_to_all | solution.py:575
  41.2 0.0 copy-start
  41.2 0.0 copy-start.8
  41.2 0.0 copy-start.6
  41.2 0.0 copy-start.7
  41.2 0.0 copy-start.5
  41.2 0.0 copy-start.4
  41.2 0.0 copy-start.1
  41.2 7.1 %all-to-all-start.1 = ((bf16[16,2,384,128]{3,2,1,0:T(8,128)(2,1)}), bf16[16,2,384,128]{3,2,1,0:T(8,128)(2,1)}, u32[]{:S(2)}, u32[]{:S(2)}) async-start(bf16[16,2,384,128]{3,2,1,0:T(8,128)(2,1)} %bitcast.28), calls=%async_computation.1 | async-start | bytes 6291456 | tf_op jit(solution)/shard_map/all_to_all | solution.py:575
  48.3 0.0 copy-done.8
  48.3 0.6 fusion
  51.6 0.0 copy-done.6
  51.6 0.0 copy-done.7
  51.7 0.0 copy-done.5
  51.7 0.1 copy.34
  51.8 0.1 copy.38
  51.9 0.1 copy.36
  52.1 0.0 copy-done.4
  52.1 0.1 copy.35
  52.2 0.0 copy-done.1
  52.3 0.2 copy.37
  52.5 0.1 maximum_divide_fusion
  52.6 0.1 pad_maximum_fusion.coef
  52.7 0.0 copy-done
  52.7 13.4 %forward.1 = (bf16[32,384,128]{2,1,0:T(8,128)(2,1)}, bf16[32,384,128]{2,1,0:T(8,128)(2,1)}, bf16[4096,384]{1,0:T(8,128)(2,1)}, bf16[8,384,128]{2,1,0:T(8,128)(2,1)S(1)}, bf16[8,384,128]{2,1,0:T(8,128)(2,1)S(1)}) custom-call(f32[6]{0:T(128)S(1)} %pad_maximum_fusion.coef, bf16[16,144,256]{2,1,0:T(8,128)(2,1)S(1)} %all-to-all-done.maps.maps_far, ...), custom_call_target="tpu_custom_call" | custom-call | flops 1000000000 | bytes 12000000 | tf_op jit(solution)/shard_map/forward/pallas_call | solution.py:447
  66.1 0.0 copy-start.2
  66.1 0.9 copy-done.2
  67.0 0.0 copy-start.3
  67.0 1.0 copy-done.3
  67.9 18.8 %coarse_node.1 = (bf16[1200,128]{1,0:T(8,128)(2,1)S(1)}, f32[384,384]{1,0:T(8,128)S(1)}, bf16[8,384,128]{2,1,0:T(8,128)(2,1)S(1)}, f32[384,256]{1,0:T(8,128)S(1)}, f32[2,16,128]{2,1,0:T(8,128)S(1)}) custom-call(f32[6]{0:T(128)S(1)} %pad_maximum_fusion.coef, bf16[8,384,128]{2,1,0:T(8,128)(2,1)S(1)} %get-tuple-element.26.pooled_depth, ...), custom_call_target="tpu_custom_call" | custom-call | flops 1000000000 | bytes 5000000 | tf_op jit(solution)/shard_map/coarse_node/pallas_call | solution.py:474
  86.7 33.4 %all-to-all-done.1 = bf16[16,2,384,128]{3,2,1,0:T(8,128)(2,1)} async-done(((bf16[16,2,384,128]{3,2,1,0:T(8,128)(2,1)}), bf16[16,2,384,128]{3,2,1,0:T(8,128)(2,1)}, u32[]{:S(2)}, u32[]{:S(2)}) %all-to-all-start.1) | async-done | bytes 3145760 | tf_op jit(solution)/shard_map/all_to_all | solution.py:575
  120.1 19.6 %backward.1 = (bf16[1792,128]{1,0:T(8,128)(2,1)S(1)}, bf16[1792,128]{1,0:T(8,128)(2,1)S(1)}) custom-call(s32[1]{0:T(128)} %bitcast.core, f32[6]{0:T(128)S(1)} %pad_maximum_fusion.coef, bf16[32,384,128]{2,1,0:T(8,128)(2,1)} %bitcast.5.cotan_far, bf16[32,384,128]{2,1,0:T(8,128)(2,1)} %get-tuple-element.23.act_far, ...), custom_call_target="tpu_custom_call" | custom-call | flops 3000000000 | bytes 16000000 | tf_op jit(solution)/shard_map/backward/pallas_call | solution.py:500
  139.8 2.3 %collective-permute-start = (bf16[1792,128]{1,0:T(8,128)(2,1)S(1)}, bf16[1792,128]{1,0:T(8,128)(2,1)S(1)}, u32[]{:S(2)}, u32[]{:S(2)}) collective-permute-start(bf16[1792,128]{1,0:T(8,128)(2,1)S(1)} %get-tuple-element.34), channel_id=1, source_target_pairs={{0,16},{16,0},{1,17},{17,1},{2,18},{18,2},{3,19},{19,3},{4,20},{20... | collective-permute-start | bytes 1376264 | tf_op jit(solution)/shard_map/ppermute | solution.py:579
  142.0 1.4 collective-permute-done
  143.5 0.1 add_convert_fusion
  143.6 16.1 %all_to_all.25 = bf16[16,112,128]{2,1,0:T(8,128)(2,1)S(1)} all-to-all(bf16[16,112,128]{2,1,0:T(8,128)(2,1)S(1)} %bitcast.29), channel_id=1, replica_groups=mesh['group'=8,'core'=2,'z'=8,'y'=2] {'group','y'}, dimensions={0} | all-to-all | bytes 917504 | tf_op jit(solution)/shard_map/all_to_all | solution.py:596
  159.7 0.1 convert_reduce_fusion
  159.8 12.1 %all_to_all.26 = bf16[8,112,128]{2,1,0:T(8,128)(2,1)S(1)} all-to-all(bf16[8,112,128]{2,1,0:T(8,128)(2,1)S(1)} %broadcast_in_dim.7), channel_id=1, replica_groups=mesh['group'=8,'core'=2,'z'=8,'y'=2] {'z'}, dimensions={0} | all-to-all | bytes 458752 | tf_op jit(solution)/shard_map/all_to_all | solution.py:585
  172.0 0.1 broadcast_in_dim.8
  172.1 11.8 %all_to_all.27 = bf16[16,112,128]{2,1,0:T(8,128)(2,1)S(1)} all-to-all(bf16[16,112,128]{2,1,0:T(8,128)(2,1)S(1)} %broadcast_in_dim.8), channel_id=1, replica_groups=mesh['group'=8,'core'=2,'z'=8,'y'=2] {'group','y'}, dimensions={0} | all-to-all | bytes 917504 | tf_op jit(solution)/shard_map/all_to_all | solution.py:585
  183.9 4.6 %collective-permute-start.1 = (bf16[1792,128]{1,0:T(8,128)(2,1)S(1)}, bf16[1792,128]{1,0:T(8,128)(2,1)S(1)}, u32[]{:S(2)}, u32[]{:S(2)}) collective-permute-start(bf16[1792,128]{1,0:T(8,128)(2,1)S(1)} %bitcast.20), channel_id=1, source_target_pairs={{0,16},{16,0},{1,17},{17,1},{2,18},{18,2},{3,19},{19,3},{4,20},{20... | collective-permute-start | bytes 1376264 | tf_op jit(solution)/shard_map/ppermute | solution.py:579
  188.5 1.4 collective-permute-done.1.other
  189.9 1.3 unpack.1
  (5 shorter events, 0.1 us)
Async XLA Ops:
  3.5 37.7 %all-to-all-start = ((bf16[16,144,256]{2,1,0:T(8,128)(2,1)}), bf16[16,144,256]{2,1,0:T(8,128)(2,1)S(1)}, u32[]{:S(2)}, u32[]{:S(2)}) async-start(bf16[16,144,256]{2,1,0:T(8,128)(2,1)} %join_maps.1), calls=%async_computation | async-start | bytes 2359296 | tf_op jit(solution)/shard_map/all_to_all | solution.py:575
  41.2 11.5 %copy-start = (bf16[16,144,256]{2,1,0:T(8,128)(2,1)}, bf16[16,144,256]{2,1,0:T(8,128)(2,1)S(1)}, u32[]{:S(2)}) copy-start(bf16[16,144,256]{2,1,0:T(8,128)(2,1)S(1)} %all-to-all-done.maps.maps_far) | copy-start | bytes 3538948
  41.2 7.1 %copy-start.8 = (f32[4]{0:T(128)S(1)}, f32[4]{0:T(128)}, u32[]{:S(2)}) copy-start(f32[4]{0:T(128)} %param.21) | copy-start | bytes 52
  41.2 10.4 %copy-start.6 = (f32[3,3,384]{2,1,0:T(4,128)S(1)}, f32[3,3,384]{2,1,0:T(4,128)}, u32[]{:S(2)}) copy-start(f32[3,3,384]{2,1,0:T(4,128)} %param.19) | copy-start | bytes 41476
  41.2 10.4 %copy-start.7 = (f32[3,3,384]{2,1,0:T(4,128)S(1)}, f32[3,3,384]{2,1,0:T(4,128)}, u32[]{:S(2)}) copy-start(f32[3,3,384]{2,1,0:T(4,128)} %param.20) | copy-start | bytes 41476
  41.2 10.5 %copy-start.5 = (bf16[80,384]{1,0:T(8,128)(2,1)S(1)}, bf16[80,384]{1,0:T(8,128)(2,1)}, u32[]{:S(2)}) copy-start(bf16[80,384]{1,0:T(8,128)(2,1)} %param.15) | copy-start | bytes 184324
  41.2 10.9 %copy-start.4 = (bf16[224,384]{1,0:T(8,128)(2,1)S(1)}, bf16[224,384]{1,0:T(8,128)(2,1)}, u32[]{:S(2)}) copy-start(bf16[224,384]{1,0:T(8,128)(2,1)} %param.16) | copy-start | bytes 516100
  41.2 11.0 %copy-start.1 = (bf16[384,384]{1,0:T(8,128)(2,1)S(1)}, bf16[384,384]{1,0:T(8,128)(2,1)}, u32[]{:S(2)}) copy-start(bf16[384,384]{1,0:T(8,128)(2,1)} %point.1) | copy-start | bytes 884740
  41.2 78.9 %all-to-all-start.1 = ((bf16[16,2,384,128]{3,2,1,0:T(8,128)(2,1)}), bf16[16,2,384,128]{3,2,1,0:T(8,128)(2,1)}, u32[]{:S(2)}, u32[]{:S(2)}) async-start(bf16[16,2,384,128]{3,2,1,0:T(8,128)(2,1)} %bitcast.28), calls=%async_computation.1 | async-start | bytes 6291456 | tf_op jit(solution)/shard_map/all_to_all | solution.py:575
  66.1 0.9 copy-start.2
  67.0 1.0 copy-start.3
  139.8 3.7 %collective-permute-start = (bf16[1792,128]{1,0:T(8,128)(2,1)S(1)}, bf16[1792,128]{1,0:T(8,128)(2,1)S(1)}, u32[]{:S(2)}, u32[]{:S(2)}) collective-permute-start(bf16[1792,128]{1,0:T(8,128)(2,1)S(1)} %get-tuple-element.34), channel_id=1, source_target_pairs={{0,16},{16,0},{1,17},{17,1},{2,18},{18,2},{3,19},{19,3},{4,20},{20... | collective-permute-start | bytes 1376264 | tf_op jit(solution)/shard_map/ppermute | solution.py:579
  183.9 6.0 %collective-permute-start.1 = (bf16[1792,128]{1,0:T(8,128)(2,1)S(1)}, bf16[1792,128]{1,0:T(8,128)(2,1)S(1)}, u32[]{:S(2)}, u32[]{:S(2)}) collective-permute-start(bf16[1792,128]{1,0:T(8,128)(2,1)S(1)} %bitcast.20), channel_id=1, source_target_pairs={{0,16},{16,0},{1,17},{17,1},{2,18},{18,2},{3,19},{19,3},{4,20},{20... | collective-permute-start | bytes 1376264 | tf_op jit(solution)/shard_map/ppermute | solution.py:579
